TPU v7x, 512 devices: a whole 4x4x16 slice. The times are simulated.
512 devices in a mesh: dp: 16 (over x, y_lo, core), mp: 32 (over z, y_hi).
Axes of the slice: x: 4, y: 4 (y_hi: 2, y_lo: 2; y = y_hi * 2 + y_lo), z: 16, core: 2. Of those that a mesh axis runs over, the one named last changes fastest.
Arguments:
- up_partials: bfloat16 [16, 32, 512, 512], P('dp', None, 'mp'), may hold values from -1.5 to 1.5
- down_partials: bfloat16 [16, 32, 512, 512], P('dp', None, 'mp'), may hold values from -1.5 to 1.5
- up_left: bfloat16 [32, 512, 512], P('mp'), may hold values from -0.25 to 0.25
- up_right: bfloat16 [32, 512, 512], P('mp'), may hold values from -0.25 to 0.25
- down_left: bfloat16 [32, 512, 512], P('mp'), may hold values from -0.25 to 0.25
- down_right: bfloat16 [32, 512, 512], P('mp'), may hold values from -0.25 to 0.25
- up_first: float32 [32, 512, 512], P('mp', 'dp'), may hold values from -4 to 4
- up_second: float32 [32, 512, 512], P('mp', 'dp'), may hold values from 0.2 to 2
- down_first: float32 [32, 512, 512], P('mp', 'dp'), may hold values from -4 to 4
- down_second: float32 [32, 512, 512], P('mp', 'dp'), may hold values from 0.2 to 2
Outputs:
- up_first_new: float32 [32, 512, 512], P('mp', 'dp')
- up_second_new: float32 [32, 512, 512], P('mp', 'dp')
- down_first_new: float32 [32, 512, 512], P('mp', 'dp')
- down_second_new: float32 [32, 512, 512], P('mp', 'dp')
- up_update: bfloat16 [32, 512, 512], P(None, 'mp', 'dp')
- down_update: bfloat16 [32, 512, 512], P(None, 'mp', 'dp')
All inputs are finite; a program needn't handle non-finite values.
Results may differ from a plain program's by a relative error of at most 0.013.
Values may be sent and summed in bfloat16 or wider, within the bound.
No kernel may reach another device: no remote copies, remote signals or barrier semaphores. Data moves between devices by JAX's collectives and lax.ppermute only.
A program may use at most 64 MiB of HBM per device.

v0:
```python
import jax
import jax.numpy as jnp
from jax import lax
from jax.sharding import PartitionSpec as P

HIGH = lax.Precision.HIGHEST
CORR_FIRST = 1.0 - 0.9**50 * 0.9**50
CORR_SECOND = 1.0 - 0.95**50 * 0.95**50


def rotate_rows(grad, left_f, right_f, first_row, width):
    left_rows = lax.dynamic_slice_in_dim(left_f, first_row, width, 2)
    half = jnp.einsum("bpr,bpq->brq", left_rows, grad, precision=HIGH)
    return jnp.einsum("brq,bqc->brc", half, right_f, precision=HIGH)


def moments(rotated, first, second):
    first_new = 0.9 * first + 0.1 * rotated
    second_new = 0.95 * second + 0.05 * rotated * rotated
    direction = (first_new / CORR_FIRST / (jnp.sqrt(second_new / CORR_SECOND) + 1e-08)).astype(
        jnp.bfloat16
    )
    return (first_new, second_new, direction)


def per_device(
    up_partials,
    down_partials,
    up_left,
    up_right,
    down_left,
    down_right,
    up_first,
    up_second,
    down_first,
    down_second,
):
    width = up_first.shape[1]
    first_row = lax.axis_index("dp") * width
    up_left_f = up_left.astype(jnp.float32)
    up_right_f = up_right.astype(jnp.float32)
    down_left_f = down_left.astype(jnp.float32)
    down_right_f = down_right.astype(jnp.float32)
    summed = (
        lax.psum(up_partials[0].astype(jnp.float32).astype(jnp.bfloat16), "dp").astype(jnp.float32),
        lax.psum(down_partials[0].astype(jnp.float32).astype(jnp.bfloat16), "dp").astype(
            jnp.float32
        ),
    )
    up_grad, down_grad = (
        lax.all_to_all(
            summed[0].astype(jnp.bfloat16), "mp", split_axis=0, concat_axis=1, tiled=True
        ).astype(jnp.float32),
        lax.all_to_all(
            summed[1].astype(jnp.bfloat16), "mp", split_axis=0, concat_axis=1, tiled=True
        ).astype(jnp.float32),
    )
    up_rot = rotate_rows(up_grad, up_left_f, up_right_f, first_row, width)
    down_rot = rotate_rows(down_grad, down_left_f, down_right_f, first_row, width)
    up_m, up_v, up_dir = moments(up_rot, up_first, up_second)
    down_m, down_v, down_dir = moments(down_rot, down_first, down_second)
    up_cols = lax.dynamic_slice_in_dim(up_right_f, first_row, width, 1)
    down_cols = lax.dynamic_slice_in_dim(down_right_f, first_row, width, 1)
    up_mid = jnp.einsum(
        "brq,bcq->brc",
        lax.all_gather(up_dir, "dp", axis=1, tiled=True).astype(jnp.float32),
        up_cols,
        precision=HIGH,
    )
    down_mid = jnp.einsum(
        "brq,bcq->brc",
        lax.all_gather(down_dir, "dp", axis=1, tiled=True).astype(jnp.float32),
        down_cols,
        precision=HIGH,
    )
    up_acc = jnp.einsum("bpr,brc->bpc", up_left_f, up_mid, precision=HIGH)
    down_acc = jnp.einsum("bpr,brc->bpc", down_left_f, down_mid, precision=HIGH)
    up_upd, down_upd = (
        lax.all_to_all(up_acc.astype(jnp.bfloat16), "mp", split_axis=1, concat_axis=0, tiled=True),
        lax.all_to_all(
            down_acc.astype(jnp.bfloat16), "mp", split_axis=1, concat_axis=0, tiled=True
        ),
    )
    return (up_m, up_v, down_m, down_v, up_upd, down_upd)


def solution(mesh):
    placed = (
        P("dp", None, "mp", None),
        P("dp", None, "mp", None),
        P("mp", None, None),
        P("mp", None, None),
        P("mp", None, None),
        P("mp", None, None),
        P("mp", "dp", None),
        P("mp", "dp", None),
        P("mp", "dp", None),
        P("mp", "dp", None),
    )
    return jax.shard_map(
        per_device,
        mesh=mesh,
        in_specs=placed,
        out_specs=(
            P("mp", "dp", None),
            P("mp", "dp", None),
            P("mp", "dp", None),
            P("mp", "dp", None),
            P(None, "mp", "dp"),
            P(None, "mp", "dp"),
        ),
        check_vma=False,
    )
```

profile of v0, /device:TPU:1, one launch (start us, length us, event | category | flops | bytes accessed | tf_op | source)
XLA Modules:
  0.0 302.9 jit_solution(8064375596884124003)
XLA Ops:
  7.2 0.7 all-reduce.3.cloned.1.call-update
  7.9 143.3 %all-reduce.3.cloned.1.call-done = (bf16[32,16,512]{2,1,0:T(8,128)(2,1)}, bf16[32,16,512]{2,1,0:T(8,128)(2,1)}) async-done(((bf16[32,16,512]{2,1,0:T(8,128)(2,1)}, bf16[32,16,512]{2,1,0:T(8,128)(2,1)}), (bf16[32,16,512]{2,1,0:T(8,128)(2,1)}, bf16[32,16,512]{2,1,0:T(8,128)(2,1)})) %all-reduce.3.cloned.1.call-update) | async-done | bytes 1048592 | tf_op jit(solution)/shard_map/psum | solution.py:45
  151.3 45.1 %all_to_all.42 = bf16[32,16,512]{2,1,0:T(8,128)(2,1)S(1)} all-to-all(bf16[32,16,512]{2,1,0:T(8,128)(2,1)} %get-tuple-element.12), channel_id=1, replica_groups=mesh['dp'=16,'mp'=32] {'mp'}, dimensions={0} | all-to-all | bytes 1048576 | tf_op jit(solution)/shard_map/all_to_all | solution.py:51
  196.3 7.3 %all-to-all-start.1 = ((bf16[32,16,512]{2,1,0:T(8,128)(2,1)}), bf16[32,16,512]{2,1,0:T(8,128)(2,1)S(1)}, u32[]{:S(2)}, u32[]{:S(2)}) async-start(bf16[32,16,512]{2,1,0:T(8,128)(2,1)} %get-tuple-element.13), calls=%async_computation.1 | async-start | bytes 1048576 | tf_op jit(solution)/shard_map/all_to_all | solution.py:54
  203.9 0.5 copy-done.4
  204.5 1.0 divide_convert_fusion.1
  205.5 19.0 %all_gather.6 = bf16[1,512,512]{2,1,0:T(8,128)(2,1)S(1)} all-gather(bf16[1,32,512]{2,1,0:T(8,128)(2,1)S(1)} %get-tuple-element.17), channel_id=1, replica_groups=mesh['dp'=16,'mp'=32] {'dp'}, dimensions={1}, use_global_device_ids=true | all-gather | bytes 557056 | tf_op jit(solution)/shard_map/all_gather | solution.py:66
  224.8 0.6 fusion
  225.5 0.5 broadcast.58
  226.1 1.4 reduce
  227.5 0.8 reshape.98
  228.3 6.0 %all-to-all-done.1 = bf16[32,16,512]{2,1,0:T(8,128)(2,1)S(1)} async-done(((bf16[32,16,512]{2,1,0:T(8,128)(2,1)}), bf16[32,16,512]{2,1,0:T(8,128)(2,1)S(1)}, u32[]{:S(2)}, u32[]{:S(2)}) %all-to-all-start.1) | async-done | bytes 524320 | tf_op jit(solution)/shard_map/all_to_all | solution.py:54
  234.2 8.8 %all-to-all-start.2 = ((bf16[32,2,256]{2,1,0:T(2,128)(2,1)}), bf16[32,2,256]{2,1,0:T(2,128)(2,1)S(1)}, u32[]{:S(2)}, u32[]{:S(2)}) async-start(bf16[32,2,256]{2,1,0:T(2,128)(2,1)} %reshape.98), calls=%async_computation.2 | async-start | bytes 65536 | tf_op jit(solution)/shard_map/all_to_all | solution.py:79
  243.1 0.3 fusion.12
  243.3 0.5 copy-done.6
  243.9 1.0 divide_convert_fusion
  245.0 18.4 %all_gather.7 = bf16[1,512,512]{2,1,0:T(8,128)(2,1)S(1)} all-gather(bf16[1,32,512]{2,1,0:T(8,128)(2,1)S(1)} %get-tuple-element.14), channel_id=1, replica_groups=mesh['dp'=16,'mp'=32] {'dp'}, dimensions={1}, use_global_device_ids=true | all-gather | bytes 557056 | tf_op jit(solution)/shard_map/all_gather | solution.py:72
  263.6 0.6 fusion.1
  264.3 1.4 reduce.1
  265.8 0.8 reshape.100
  266.5 14.9 %all-to-all-start.3 = ((bf16[32,2,256]{2,1,0:T(2,128)(2,1)}), bf16[32,2,256]{2,1,0:T(2,128)(2,1)S(1)}, u32[]{:S(2)}, u32[]{:S(2)}) async-start(bf16[32,2,256]{2,1,0:T(2,128)(2,1)} %reshape.100), calls=%async_computation.3 | async-start | bytes 65536 | tf_op jit(solution)/shard_map/all_to_all | solution.py:80
  281.6 0.7 copy.22
  282.3 13.0 %all-to-all-done.3 = bf16[32,2,256]{2,1,0:T(2,128)(2,1)S(1)} async-done(((bf16[32,2,256]{2,1,0:T(2,128)(2,1)}), bf16[32,2,256]{2,1,0:T(2,128)(2,1)S(1)}, u32[]{:S(2)}, u32[]{:S(2)}) %all-to-all-start.3) | async-done | bytes 32800 | tf_op jit(solution)/shard_map/all_to_all | solution.py:80
  295.4 0.7 copy.23
  (23 shorter events, 1.6 us)
Async XLA Ops:
  7.2 196.8 %copy-start = (bf16[1,512,512]{2,1,0:T(8,128)(2,1)S(1)}, bf16[1,512,512]{2,1,0:T(8,128)(2,1)}, u32[]{:S(2)}) copy-start(bf16[1,512,512]{2,1,0:T(8,128)(2,1)} %param.13) | copy-start | bytes 1572868
  7.2 144.1 %all-reduce.3.cloned.1.call-start = ((), (), s32[]{:S(2)}) async-start(), calls=%async_computation.4 | async-start | bytes 2097152 | tf_op jit(solution)/shard_map/psum | solution.py:45
  196.3 7.3 %copy-start.1 = (bf16[1,512,512]{2,1,0:T(8,128)(2,1)S(1)}, bf16[1,512,512]{2,1,0:T(8,128)(2,1)}, u32[]{:S(2)}) copy-start(bf16[1,512,512]{2,1,0:T(8,128)(2,1)} %param.12) | copy-start | bytes 1572868
  196.3 37.9 %all-to-all-start.1 = ((bf16[32,16,512]{2,1,0:T(8,128)(2,1)}), bf16[32,16,512]{2,1,0:T(8,128)(2,1)S(1)}, u32[]{:S(2)}, u32[]{:S(2)}) async-start(bf16[32,16,512]{2,1,0:T(8,128)(2,1)} %get-tuple-element.13), calls=%async_computation.1 | async-start | bytes 1048576 | tf_op jit(solution)/shard_map/all_to_all | solution.py:54
  203.6 0.8 copy-start.4
  203.6 0.9 copy-start.5
  225.4 17.7 %copy-start.2 = (bf16[1,512,512]{2,1,0:T(8,128)(2,1)S(1)}, bf16[1,512,512]{2,1,0:T(8,128)(2,1)}, u32[]{:S(2)}) copy-start(bf16[1,512,512]{2,1,0:T(8,128)(2,1)} %param.14) | copy-start | bytes 1572868
  227.5 15.8 %copy-start.3 = (bf16[1,512,512]{2,1,0:T(8,128)(2,1)S(1)}, bf16[1,512,512]{2,1,0:T(8,128)(2,1)}, u32[]{:S(2)}) copy-start(bf16[1,512,512]{2,1,0:T(8,128)(2,1)} %param.15) | copy-start | bytes 1572868
  234.2 32.3 %all-to-all-start.2 = ((bf16[32,2,256]{2,1,0:T(2,128)(2,1)}), bf16[32,2,256]{2,1,0:T(2,128)(2,1)S(1)}, u32[]{:S(2)}, u32[]{:S(2)}) async-start(bf16[32,2,256]{2,1,0:T(2,128)(2,1)} %reshape.98), calls=%async_computation.2 | async-start | bytes 65536 | tf_op jit(solution)/shard_map/all_to_all | solution.py:79
  243.0 0.8 copy-start.6
  243.0 0.9 copy-start.7
  266.5 28.7 %all-to-all-start.3 = ((bf16[32,2,256]{2,1,0:T(2,128)(2,1)}), bf16[32,2,256]{2,1,0:T(2,128)(2,1)S(1)}, u32[]{:S(2)}, u32[]{:S(2)}) async-start(bf16[32,2,256]{2,1,0:T(2,128)(2,1)} %reshape.100), calls=%async_computation.3 | async-start | bytes 65536 | tf_op jit(solution)/shard_map/all_to_all | solution.py:80
Sparse Core Ops, SparseCore 0:
  11.0 140.2 all-reduce.2
where the time goes:
time: 303 us
  waiting for transfers between devices  163 us (54%)
  blocking collectives  82.4 us (27%)
  starting transfers between devices  31 us (10%)
  between operations  14.2 us (5%)
  local copies, waits for them, and re-layouts  5.18 us (2%)
  matrix products  4.31 us (1%)
    psum x1, waiting for transfers between devices, per_device(): lax.psum(up_partials[0].astype(jnp.float32).astype(jnp.bfloat16), 'dp')  143 us
    all_to_all x1, blocking collectives, per_device(): lax.all_to_all(summed[0].astype(jnp.bfloat16), 'mp', split_axis=0, concat...  45.1 us
    all_gather x1, blocking collectives, per_device(): lax.all_gather(up_dir, 'dp', axis=1, tiled=True).astype(jnp.float32)  19 us
    all_gather x1, blocking collectives, per_device(): lax.all_gather(down_dir, 'dp', axis=1, tiled=True).astype(jnp.float32)  18.4 us
    all_to_all x1, starting transfers between devices, per_device(): lax.all_to_all(down_acc.astype(jnp.bfloat16), 'mp', split_axis=1, concat_...  14.9 us
    all_to_all x1, waiting for transfers between devices, per_device(): lax.all_to_all(down_acc.astype(jnp.bfloat16), 'mp', split_axis=1, concat_...  13 us
    all_to_all x1, starting transfers between devices, per_device(): lax.all_to_all(up_acc.astype(jnp.bfloat16), 'mp', split_axis=1, concat_ax...  8.76 us
    all_to_all x1, starting transfers between devices, per_device(): lax.all_to_all(summed[1].astype(jnp.bfloat16), 'mp', split_axis=0, concat...  7.26 us
  transfers between devices with their start and end apart: 4, of which 3 were waited for; matrix products, arithmetic and copies ran while one was open for 3% of the time, Pallas kernels for 0%

commit v1 on v0

v1 whole, which is shorter than its diff:
```python
import jax
import jax.numpy as jnp
from jax import lax
from jax.sharding import PartitionSpec as P

CORR_FIRST = 1.0 - 0.9**50 * 0.9**50
CORR_SECOND = 1.0 - 0.95**50 * 0.95**50
BF = jnp.bfloat16
F32 = jnp.float32


def exchange(x, axis):
    return lax.all_to_all(x, axis, 0, 0, tiled=True)


def moments(rotated, first, second):
    first_new = 0.9 * first + 0.1 * rotated
    second_new = 0.95 * second + 0.05 * rotated * rotated
    direction = first_new / CORR_FIRST / (jnp.sqrt(second_new / CORR_SECOND) + 1e-08)
    return first_new, second_new, direction.astype(BF)


def per_device(
    up_partials,
    down_partials,
    up_left,
    up_right,
    down_left,
    down_right,
    up_first,
    up_second,
    down_first,
    down_second,
):
    me = lax.axis_index("dp")
    proj, part = me % 2, (me // 2) % 2

    both = jnp.stack([up_partials[0], down_partials[0]])
    chunks = both.reshape(2, 32, 2, 8, 4, 128).transpose(4, 2, 0, 1, 3, 5).reshape(16, 32, 8, 128)
    summed = jnp.sum(exchange(chunks, "dp").astype(F32), axis=0).astype(BF)
    grad = exchange(summed, "mp").reshape(256, 128)

    left = jnp.where(proj == 0, up_left[0], down_left[0]).reshape(32, 2, 8, 512)
    left = lax.dynamic_index_in_dim(left, part, 1, keepdims=False).reshape(256, 512)
    half = jnp.einsum("pr,pq->rq", left, grad, preferred_element_type=F32)
    half = exchange(half.astype(BF).reshape(16, 32, 128), "dp")
    half = jnp.sum(half.reshape(4, 2, 2, 32, 128).astype(F32), axis=1).astype(BF)

    outs, mids = [], []
    for k, (right, first, second) in enumerate(
        ((up_right, up_first, up_second), (down_right, down_first, down_second))
    ):
        rows = half[:, k].transpose(1, 0, 2).reshape(32, 512)
        rotated = jnp.einsum("rq,qc->rc", rows, right[0], preferred_element_type=F32)
        first_new, second_new, direction = moments(rotated, first[0], second[0])
        outs += [first_new[None], second_new[None]]
        mid = jnp.einsum("rq,cq->rc", direction, right[0], preferred_element_type=F32)
        mids.append(mid.astype(BF).reshape(32, 16, 32).transpose(1, 0, 2))
    mid = exchange(jnp.concatenate(mids, axis=2), "dp").reshape(512, 64)

    zero = jnp.zeros((512, 32), BF)
    up_mid, down_mid = mid[:, :32], mid[:, 32:]
    packed = 0.0
    for part_at in range(2):
        for k, (own, block) in enumerate(((up_mid, up_left), (down_mid, down_left))):
            at = 2 * part_at + k
            lanes = jnp.concatenate([own if at == j else zero for j in range(4)], axis=1)
            rows = block[0].reshape(32, 2, 8, 512)[:, part_at].reshape(256, 512)
            packed = packed + jnp.einsum("pr,rc->pc", rows, lanes, preferred_element_type=F32)
    packed = exchange(packed.astype(BF).reshape(32, 8, 128), "mp").reshape(32, 8, 2, 2, 32)
    packed = packed.transpose(3, 0, 2, 1, 4).reshape(2, 32, 16, 32)
    return (*outs, packed[0], packed[1])


def solution(mesh):
    blocks, rows = P("mp", None, None), P("mp", "dp", None)
    partials, update = P("dp", None, "mp", None), P(None, "mp", "dp")
    return jax.shard_map(
        per_device,
        mesh=mesh,
        in_specs=(partials, partials, blocks, blocks, blocks, blocks, rows, rows, rows, rows),
        out_specs=(rows, rows, rows, rows, update, update),
        check_vma=False,
    )
```

time: 303 us -> 103 us (0.34)
  waiting for transfers between devices: 163 us -> 27.3 us
  blocking collectives: 82.4 us -> 44.9 us
  between operations: 14.2 us -> 0.86 us
  starting transfers between devices: 31 us -> 18.6 us
    psum x1 -> x0, waiting for transfers between devices: 143 us -> none  [per_device(): lax.psum(up_partials[0].astype(jnp.float32).astype(jnp.bfloat16), 'dp')]
    all_gather x2 -> x0, blocking collectives: 37.3 us -> none  [the longest x1 19 us: per_device(): lax.all_gather(up_dir, 'dp', axis=1, tiled=True).astype(jnp.float32)]
    all_to_all x3 -> x2, starting transfers between devices: 30.9 us -> 18.6 us  [exchange(): return lax.all_to_all(x, axis, 0, 0, tiled=True)]
    all_to_all x3 -> x2, waiting for transfers between devices: 18.9 us -> 27.3 us  [exchange(): return lax.all_to_all(x, axis, 0, 0, tiled=True)]
    all_to_all x1 -> x3, blocking collectives: 45.1 us -> 44.9 us  [exchange(): return lax.all_to_all(x, axis, 0, 0, tiled=True)]
  transfers between devices with their start and end apart: 4 -> 2, of which waited for: 3 -> 2; matrix products, arithmetic and copies ran while one was open for 3% -> 1% of each run, Pallas kernels for 0% -> 0%
where the time goes in v1:
time: 103 us
  blocking collectives  44.9 us (44%)
  waiting for transfers between devices  27.3 us (27%)
  starting transfers between devices  18.6 us (18%)
  local copies, waits for them, and re-layouts  5.69 us (6%)
  other arithmetic  2.98 us (3%)
  matrix products  2.35 us (2%)
    all_to_all x3, blocking collectives, exchange(): return lax.all_to_all(x, axis, 0, 0, tiled=True)  44.9 us
    all_to_all x2, waiting for transfers between devices, exchange(): return lax.all_to_all(x, axis, 0, 0, tiled=True)  27.3 us
    all_to_all x2, starting transfers between devices, exchange(): return lax.all_to_all(x, axis, 0, 0, tiled=True)  18.6 us
    unnamed x19, local copies, waits for them, and re-layouts  2.3 us
  transfers between devices with their start and end apart: 2, of which 2 were waited for; matrix products, arithmetic and copies ran while one was open for 1% of the time, Pallas kernels for 0%

profile of v1, /device:TPU:1, one launch (start us, length us, event | category | flops | bytes accessed | tf_op | source)
XLA Modules:
  0.0 102.7 jit_solution(6239120832211565030)
XLA Ops:
  0.6 1.4 %maximum_bitcast_fusion = bf16[4,2,2,32,8,128]{5,4,0,1,3,2:T(8,128)(2,1)S(1)} fusion(bf16[1,32,16,512]{3,2,1,0:T(8,128)(2,1)} %param.11, bf16[1,32,16,512]{3,2,1,0:T(8,128)(2,1)} %param.10), kind=kLoop, calls=%fused_computation.8 | loop fusion | flops 524288 | bytes 2097152 | tf_op jit(solution)/shard_map/transpose | solution.py:39
  2.0 0.3 copy.28
  2.3 24.6 %all_to_all.25 = bf16[16,32,8,128]{3,2,1,0:T(8,128)(2,1)S(1)} all-to-all(bf16[16,32,8,128]{3,2,1,0:T(8,128)(2,1)S(1)} %bitcast.104), channel_id=1, replica_groups=mesh['dp'=16,'mp'=32] {'dp'}, dimensions={0} | all-to-all | bytes 2097152 | tf_op jit(solution)/shard_map/all_to_all | solution.py:13
  26.9 0.8 reduce_sum.24
  27.7 14.8 %all-to-all-start.1 = ((bf16[32,8,128]{2,1,0:T(8,128)(2,1)}), bf16[32,8,128]{2,1,0:T(8,128)(2,1)S(1)}, u32[]{:S(2)}, u32[]{:S(2)}) async-start(bf16[32,8,128]{2,1,0:T(8,128)(2,1)} %reduce_sum.24), calls=%async_computation.1 | async-start | bytes 131072 | tf_op jit(solution)/shard_map/all_to_all | solution.py:13
  42.5 14.0 %all-to-all-done.1 = bf16[32,8,128]{2,1,0:T(8,128)(2,1)S(1)} async-done(((bf16[32,8,128]{2,1,0:T(8,128)(2,1)}), bf16[32,8,128]{2,1,0:T(8,128)(2,1)S(1)}, u32[]{:S(2)}, u32[]{:S(2)}) %all-to-all-start.1) | async-done | bytes 65568 | tf_op jit(solution)/shard_map/all_to_all | solution.py:13
  56.6 0.3 convolution_convert_fusion
  56.8 11.5 %all_to_all.26 = bf16[16,32,128]{2,1,0:T(8,128)(2,1)S(1)} all-to-all(bf16[16,32,128]{2,1,0:T(8,128)(2,1)S(1)} %bitcast.114), channel_id=1, replica_groups=mesh['dp'=16,'mp'=32] {'dp'}, dimensions={0} | all-to-all | bytes 262144 | tf_op jit(solution)/shard_map/all_to_all | solution.py:13
  68.6 0.6 copy-done.6
  69.3 0.2 convolution_convert_fusion.2
  69.6 0.6 copy-done.1
  70.5 0.7 copy-done.4
  71.2 0.2 convolution_convert_fusion.1
  71.9 8.8 %all_to_all.27 = bf16[16,2,1024]{2,1,0:T(2,128)(2,1)S(1)} all-to-all(bf16[16,2,1024]{2,1,0:T(2,128)(2,1)S(1)} %reshape.81), channel_id=1, replica_groups=mesh['dp'=16,'mp'=32] {'dp'}, dimensions={0} | all-to-all | bytes 131072 | tf_op jit(solution)/shard_map/all_to_all | solution.py:13
  81.2 0.3 convolution_add_fusion.2
  81.6 0.3 convolution_add_fusion.1
  81.9 0.3 fusion.1
  82.2 0.7 copy.33
  83.0 3.9 %all-to-all-start.4 = ((bf16[32,8,128]{2,1,0:T(8,128)(2,1)}), bf16[32,8,128]{2,1,0:T(8,128)(2,1)S(1)}, u32[]{:S(2)}, u32[]{:S(2)}) async-start(bf16[32,8,128]{2,1,0:T(8,128)(2,1)} %bitcast.31), calls=%async_computation.4 | async-start | bytes 131072 | tf_op jit(solution)/shard_map/all_to_all | solution.py:13
  86.8 0.7 fusion.41
  87.5 13.3 %all-to-all-done.4 = bf16[32,8,128]{2,1,0:T(8,128)(2,1)S(1)} async-done(((bf16[32,8,128]{2,1,0:T(8,128)(2,1)}), bf16[32,8,128]{2,1,0:T(8,128)(2,1)S(1)}, u32[]{:S(2)}, u32[]{:S(2)}) %all-to-all-start.4) | async-done | bytes 65568 | tf_op jit(solution)/shard_map/all_to_all | solution.py:13
  101.0 0.4 fusion.63
  101.4 0.7 copy.50
  102.0 0.7 copy.51
  (28 shorter events, 1.8 us)
Async XLA Ops:
  0.6 67.7 %copy-start = (bf16[1,512,512]{2,1,0:T(8,128)(2,1)S(1)}, bf16[1,512,512]{2,1,0:T(8,128)(2,1)}, u32[]{:S(2)}) copy-start(bf16[1,512,512]{2,1,0:T(8,128)(2,1)} %param.13) | copy-start | bytes 1572868
  26.9 29.6 %copy-start.2 = (bf16[1,512,512]{2,1,0:T(8,128)(2,1)S(1)}, bf16[1,512,512]{2,1,0:T(8,128)(2,1)}, u32[]{:S(2)}) copy-start(bf16[1,512,512]{2,1,0:T(8,128)(2,1)} %param.12) | copy-start | bytes 1572868
  26.9 29.7 %copy-start.3 = (bf16[1,512,512]{2,1,0:T(8,128)(2,1)S(1)}, bf16[1,512,512]{2,1,0:T(8,128)(2,1)}, u32[]{:S(2)}) copy-start(bf16[1,512,512]{2,1,0:T(8,128)(2,1)} %param.14) | copy-start | bytes 1572868
  27.7 28.9 %all-to-all-start.1 = ((bf16[32,8,128]{2,1,0:T(8,128)(2,1)}), bf16[32,8,128]{2,1,0:T(8,128)(2,1)S(1)}, u32[]{:S(2)}, u32[]{:S(2)}) async-start(bf16[32,8,128]{2,1,0:T(8,128)(2,1)} %reduce_sum.24), calls=%async_computation.1 | async-start | bytes 131072 | tf_op jit(solution)/shard_map/all_to_all | solution.py:13
  68.4 0.8 copy-start.6
  68.4 0.9 copy-start.7
  69.2 1.0 %copy-start.1 = (bf16[1,512,512]{2,1,0:T(8,128)(2,1)S(1)}, bf16[1,512,512]{2,1,0:T(8,128)(2,1)}, u32[]{:S(2)}) copy-start(bf16[1,512,512]{2,1,0:T(8,128)(2,1)} %param.15) | copy-start | bytes 1572868
  70.3 0.8 copy-start.4
  70.3 0.9 copy-start.5
  83.0 17.9 %all-to-all-start.4 = ((bf16[32,8,128]{2,1,0:T(8,128)(2,1)}), bf16[32,8,128]{2,1,0:T(8,128)(2,1)S(1)}, u32[]{:S(2)}, u32[]{:S(2)}) async-start(bf16[32,8,128]{2,1,0:T(8,128)(2,1)} %bitcast.31), calls=%async_computation.4 | async-start | bytes 131072 | tf_op jit(solution)/shard_map/all_to_all | solution.py:13

commit v2 on v1

v2 whole, which is shorter than its diff:
```python
import jax
import jax.numpy as jnp
from jax import lax
from jax.experimental import pallas as pl
from jax.experimental.pallas import tpu as pltpu
from jax.sharding import Mesh
from jax.sharding import PartitionSpec as P

CORR_FIRST = 1.0 - 0.9**50 * 0.9**50
CORR_SECOND = 1.0 - 0.95**50 * 0.95**50
BF = jnp.bfloat16
F32 = jnp.float32
DP = ("x", "y", "core")
PARAMS = pltpu.CompilerParams(vmem_limit_bytes=16 * 2**20)


def exchange(x, axis):
    return lax.all_to_all(x, axis, 0, 0, tiled=True)


def call(kernel, out_shape, *args):
    return pl.pallas_call(kernel, out_shape=out_shape, compiler_params=PARAMS)(*args)


def chunk_kernel(up_ref, down_ref, got_ref, out_ref):
    def chunks(own_ref):
        for at in range(4):
            lanes = pl.ds(128 * at, 128)
            total = own_ref[0, :, :, lanes].astype(F32) + got_ref[:, :, lanes].astype(F32)
            total = total.reshape(16, 2, 2, 8, 128)
            for half in range(2):
                out_ref[2 * at + half] = total[:, :, half].reshape(16, 16, 128).astype(BF)

    core = lax.axis_index("core")

    @pl.when(core == 0)
    def _():
        chunks(up_ref)

    @pl.when(core == 1)
    def _():
        chunks(down_ref)


def middle_kernel(
    half_ref,
    up_right,
    down_right,
    up_first,
    up_second,
    down_first,
    down_second,
    up_first_new,
    up_second_new,
    down_first_new,
    down_second_new,
    mid_ref,
):
    mids = []
    for k, (right, first, second, first_out, second_out) in enumerate(
        (
            (up_right, up_first, up_second, up_first_new, up_second_new),
            (down_right, down_first, down_second, down_first_new, down_second_new),
        )
    ):
        tiles = [
            (half_ref[4 * at + k].astype(F32) + half_ref[4 * at + 2 + k].astype(F32)).astype(BF)
            for at in range(4)
        ]
        rows = jnp.concatenate(tiles, axis=1)
        rotated = jnp.dot(rows, right[0], preferred_element_type=F32)
        first_new = 0.9 * first[0] + 0.1 * rotated
        second_new = 0.95 * second[0] + 0.05 * rotated * rotated
        first_out[0] = first_new
        second_out[0] = second_new
        direction = first_new / CORR_FIRST / (jnp.sqrt(second_new / CORR_SECOND) + 1e-08)
        mids.append(
            lax.dot_general(
                direction.astype(BF),
                right[0],
                (((1,), (1,)), ((), ())),
                preferred_element_type=F32,
            )
        )
    lane = lax.broadcasted_iota(jnp.int32, (16, 128), 1)
    for at in range(4):
        pieces = [
            mids[k][16 * rh : 16 * rh + 16, 128 * at : 128 * at + 128]
            for rh in range(2)
            for k in range(2)
        ]
        for w in range(4):
            rolled = [
                piece if g == w else pltpu.roll(piece, (32 * (g - w)) % 128, 1)
                for g, piece in enumerate(pieces)
            ]
            packed = jnp.where(
                lane < 64,
                jnp.where(lane < 32, rolled[0], rolled[1]),
                jnp.where(lane < 96, rolled[2], rolled[3]),
            )
            mid_ref[4 * at + w] = packed.astype(BF)


def back_kernel(mid_ref, up_left, down_left, out_ref):
    mid = mid_ref[...].astype(F32)
    other = pltpu.roll(mid.reshape(256, 128), 64, 1).reshape(16, 16, 128)
    mid = jnp.stack([mid, other], axis=1).reshape(512, 128).astype(BF)
    up = jnp.dot(up_left[0], mid, preferred_element_type=F32)
    down = jnp.dot(down_left[0], mid, preferred_element_type=F32)
    lane = lax.broadcasted_iota(jnp.int32, (512, 128), 1)
    both = jnp.where(lane < 32, up, down).reshape(32, 2, 8, 128)
    top = both[:, 0].reshape(256, 128)
    low = pltpu.roll(both[:, 1].reshape(256, 128), 64, 1)
    lane = lax.broadcasted_iota(jnp.int32, (256, 128), 1)
    out_ref[...] = jnp.where(lane < 64, top, low).reshape(16, 16, 128).astype(BF)


def unpack_kernel(got_ref, up_ref, down_ref):
    got = got_ref[...].astype(F32).reshape(256, 128)
    low = pltpu.roll(got, 64, 1)
    rows = jnp.stack([got.reshape(32, 8, 128), low.reshape(32, 8, 128)], axis=1)
    rows = rows.reshape(512, 128)
    up_ref[...] = rows[:, :32].reshape(32, 16, 32).astype(BF)
    down_ref[...] = pltpu.roll(rows, 96, 1)[:, :32].reshape(32, 16, 32).astype(BF)


def per_device(
    up_partials,
    down_partials,
    up_left,
    up_right,
    down_left,
    down_right,
    up_first,
    up_second,
    down_first,
    down_second,
):
    core, part = lax.axis_index("core"), lax.axis_index("y")

    sent = jnp.where(core == 0, down_partials[0], up_partials[0])
    got = lax.ppermute(sent, "core", [(0, 1), (1, 0)])
    chunks = call(
        chunk_kernel,
        jax.ShapeDtypeStruct((8, 16, 16, 128), BF),
        up_partials,
        down_partials,
        got,
    )
    summed = jnp.sum(exchange(chunks, ("x", "y")).astype(F32), axis=0).astype(BF)
    grad = exchange(summed.reshape(32, 8, 128), "mp").reshape(256, 128)

    left = jnp.where(core == 0, up_left[0], down_left[0]).reshape(32, 2, 8, 512)
    left = lax.dynamic_index_in_dim(left, part, 1, keepdims=False).reshape(256, 512)
    half = jnp.einsum("pr,pq->rq", left, grad, preferred_element_type=F32)
    half = exchange(half.astype(BF).reshape(16, 32, 128), DP)

    rows = jax.ShapeDtypeStruct((1, 32, 512), F32)
    *moments, mid = call(
        middle_kernel,
        [rows] * 4 + [jax.ShapeDtypeStruct((16, 16, 128), BF)],
        half,
        up_right,
        down_right,
        up_first,
        up_second,
        down_first,
        down_second,
    )
    mid = exchange(mid, DP)
    packed = call(
        back_kernel, jax.ShapeDtypeStruct((16, 16, 128), BF), mid, up_left, down_left
    )
    packed = exchange(packed.reshape(32, 8, 128), "mp").reshape(16, 16, 128)
    updates = call(unpack_kernel, [jax.ShapeDtypeStruct((32, 16, 32), BF)] * 2, packed)
    return (*moments, *updates)


def solution(mesh):
    mesh = Mesh(mesh.devices.reshape(4, 2, 2, 32), ("x", "y", "core", "mp"))
    blocks, rows = P("mp", None, None), P("mp", DP, None)
    partials, update = P(DP, None, "mp", None), P(None, "mp", DP)
    return jax.shard_map(
        per_device,
        mesh=mesh,
        in_specs=(partials, partials, blocks, blocks, blocks, blocks, rows, rows, rows, rows),
        out_specs=(rows, rows, rows, rows, update, update),
        check_vma=False,
    )
```

time: 103 us -> 95.4 us (0.926)
  starting transfers between devices: 18.6 us -> 26.2 us
  blocking collectives: 44.9 us -> 37.4 us
  local copies, waits for them, and re-layouts: 5.69 us -> 0.06 us
  Pallas kernels: 0 us -> 3.77 us
  waiting for transfers between devices: 27.3 us -> 24.6 us
  matrix products: 2.35 us -> 0.27 us
    ppermute x0 -> x1, starting transfers between devices: none -> 8.78 us  [per_device(): got = lax.ppermute(sent, 'core', [(0, 1), (1, 0)])]
    all_to_all x3, blocking collectives: 44.9 us -> 37.4 us  [exchange(): return lax.all_to_all(x, axis, 0, 0, tiled=True)]
    all_to_all x2, waiting for transfers between devices: 27.3 us -> 23.1 us  [exchange(): return lax.all_to_all(x, axis, 0, 0, tiled=True)]
    pallas_call x0 -> x4, Pallas kernels: none -> 3.77 us  [call(): pl.pallas_call(kernel, out_shape=out_shape, compiler_params=PARAMS)(*args)]
    unnamed x19 -> x20, local copies, waits for them, and re-layouts: 2.3 us -> 0.06 us
    dot_general x8 -> x0, matrix products: 2.07 us -> none  [the longest x4 1.23 us: per_device(): jnp.einsum('pr,rc->pc', rows, lanes, preferred_element_type=F32)]
    slice x4 -> x0, local copies, waits for them, and re-layouts: 1.84 us -> none  [the longest x3 1.72 us: per_device(): return (*outs, packed[0], packed[1])]
    ppermute x0 -> x1, waiting for transfers between devices: none -> 1.51 us  [per_device(): got = lax.ppermute(sent, 'core', [(0, 1), (1, 0)])]
  transfers between devices with their start and end apart: 2 -> 3, of which waited for: 2 -> 3; matrix products, arithmetic and copies ran while one was open for 1% -> 0% of each run, Pallas kernels for 0% -> 0%
where the time goes in v2:
time: 95.4 us; the launch traced here: 95 us
  blocking collectives  37.4 us (39%)
  starting transfers between devices  26.2 us (27%)
  waiting for transfers between devices  24.6 us (26%)
  Pallas kernels  3.77 us (4%)
  other arithmetic  1.96 us (2%)
    all_to_all x3, blocking collectives, exchange(): return lax.all_to_all(x, axis, 0, 0, tiled=True)  37.4 us
    all_to_all x2, waiting for transfers between devices, exchange(): return lax.all_to_all(x, axis, 0, 0, tiled=True)  23.1 us
    all_to_all x2, starting transfers between devices, exchange(): return lax.all_to_all(x, axis, 0, 0, tiled=True)  17.4 us
    ppermute x1, starting transfers between devices, per_device(): got = lax.ppermute(sent, 'core', [(0, 1), (1, 0)])  8.78 us
    pallas_call x4, Pallas kernels, call(): pl.pallas_call(kernel, out_shape=out_shape, compiler_params=PARAMS)(*args)  3.77 us
  transfers between devices with their start and end apart: 3, of which 3 were waited for; matrix products, arithmetic and copies ran while one was open for 0% of the time, Pallas kernels for 0%

profile of v2, /device:TPU:1, one launch (start us, length us, event | category | flops | bytes accessed | tf_op | source)
XLA Modules:
  0.0 95.0 jit_solution(16774722696056185486)
XLA Ops:
  0.7 1.2 %select_bitcast_fusion = bf16[32,16,512]{2,1,0:T(8,128)(2,1)S(1)} fusion(bf16[1,32,16,512]{3,2,1,0:T(8,128)(2,1)} %down_ref.1, bf16[1,32,16,512]{3,2,1,0:T(8,128)(2,1)} %up_ref.1, pred[]{:T(512)S(6)} %eq.4), kind=kLoop, calls=%fused_computation.1 | loop fusion | flops 262144 | bytes 1572865 | tf_op jit(solution)/shard_map/jit(_where)/select_n | solution.py:142
  1.9 8.8 %collective-permute-start = (bf16[32,16,512]{2,1,0:T(8,128)(2,1)S(1)}, bf16[32,16,512]{2,1,0:T(8,128)(2,1)S(1)}, u32[]{:S(2)}, u32[]{:S(2)}) collective-permute-start(bf16[32,16,512]{2,1,0:T(8,128)(2,1)S(1)} %select_bitcast_fusion), channel_id=1, source_target_pairs={{0,32},{32,0},{1,33},{33,1},{2,34},{34,2},{3,35},{35,3},{4,36},{36... | collective-permute-start | bytes 1572872 | tf_op jit(solution)/shard_map/ppermute | solution.py:143
  10.6 1.5 %collective-permute-done.got_ref = bf16[32,16,512]{2,1,0:T(8,128)(2,1)S(1)} collective-permute-done((bf16[32,16,512]{2,1,0:T(8,128)(2,1)S(1)}, bf16[32,16,512]{2,1,0:T(8,128)(2,1)S(1)}, u32[]{:S(2)}, u32[]{:S(2)}) %collective-permute-start) | collective-permute-done | bytes 524320 | tf_op jit(solution)/shard_map/ppermute | solution.py:143
  12.2 1.0 %shard_map.145 = bf16[8,16,16,128]{3,2,1,0:T(8,128)(2,1)} custom-call(bf16[1,32,16,512]{3,2,1,0:T(8,128)(2,1)S(1)} %copy-done.2, bf16[1,32,16,512]{3,2,1,0:T(8,128)(2,1)S(1)} %copy-done.3, bf16[32,16,512]{2,1,0:T(8,128)(2,1)S(1)} %collective-permute-done.got_ref), custom_call_target="tpu_custom_call" | custom-call | tf_op jit(solution)/shard_map/pallas_call | solution.py:22
  13.1 3.6 %all-to-all-start = ((bf16[8,16,16,128]{3,2,1,0:T(8,128)(2,1)}), bf16[8,16,16,128]{3,2,1,0:T(8,128)(2,1)S(1)}, u32[]{:S(2)}, u32[]{:S(2)}) async-start(bf16[8,16,16,128]{3,2,1,0:T(8,128)(2,1)} %shard_map.145), calls=%async_computation | async-start | bytes 1048576 | tf_op jit(solution)/shard_map/all_to_all | solution.py:18
  16.8 0.0 copy-start
  16.8 9.1 %all-to-all-done = bf16[8,16,16,128]{3,2,1,0:T(8,128)(2,1)S(1)} async-done(((bf16[8,16,16,128]{3,2,1,0:T(8,128)(2,1)}), bf16[8,16,16,128]{3,2,1,0:T(8,128)(2,1)S(1)}, u32[]{:S(2)}, u32[]{:S(2)}) %all-to-all-start) | async-done | bytes 524320 | tf_op jit(solution)/shard_map/all_to_all | solution.py:18
  25.9 0.7 reduce_sum.12
  26.6 13.8 %all-to-all-start.1 = ((bf16[32,8,128]{2,1,0:T(8,128)(2,1)}), bf16[32,8,128]{2,1,0:T(8,128)(2,1)S(1)}, u32[]{:S(2)}, u32[]{:S(2)}) async-start(bf16[32,8,128]{2,1,0:T(8,128)(2,1)} %bitcast.3), calls=%async_computation.1 | async-start | bytes 131072 | tf_op jit(solution)/shard_map/all_to_all | solution.py:18
  40.4 0.0 copy-start.5
  40.4 0.0 copy-start.9
  40.4 0.1 broadcast_select_fusion
  40.5 0.0 copy-start.4
  40.5 14.0 %all-to-all-done.1 = bf16[32,8,128]{2,1,0:T(8,128)(2,1)S(1)} async-done(((bf16[32,8,128]{2,1,0:T(8,128)(2,1)}), bf16[32,8,128]{2,1,0:T(8,128)(2,1)S(1)}, u32[]{:S(2)}, u32[]{:S(2)}) %all-to-all-start.1) | async-done | bytes 65568 | tf_op jit(solution)/shard_map/all_to_all | solution.py:18
  54.5 0.3 convolution_convert_fusion
  54.7 0.0 copy-start.6
  54.8 0.0 copy-start.7
  54.8 0.0 copy-start.8
  54.8 11.6 %all_to_all.25.half_ref = bf16[16,32,128]{2,1,0:T(8,128)(2,1)S(1)} all-to-all(bf16[16,32,128]{2,1,0:T(8,128)(2,1)S(1)} %bitcast.16), channel_id=1, replica_groups=mesh['x'=4,'y'=2,'core'=2,'mp'=32] {'x','y','core'}, dimensions={0} | all-to-all | bytes 262144 | tf_op jit(solution)/shard_map/all_to_all | solution.py:18
  66.4 1.4 %shard_map.146 = (f32[1,32,512]{2,1,0:T(8,128)}, f32[1,32,512]{2,1,0:T(8,128)}, f32[1,32,512]{2,1,0:T(8,128)}, f32[1,32,512]{2,1,0:T(8,128)}, bf16[16,16,128]{2,1,0:T(8,128)(2,1)S(1)}) custom-call(bf16[16,32,128]{2,1,0:T(8,128)(2,1)S(1)} %all_to_all.25.half_ref, bf16[1,512,512]{2,1,0:T(8,128)(2,1)S(1)} %copy-done.4, bf16[1,512,512]{2,1,0:T(8,128)(2,1)S(1)} %copy-done.5, ...), custom_call_target="tpu_custom_call" | custom-call | tf_op jit(solution)/shard_map/pallas_call | solution.py:22
  67.8 8.7 %all_to_all.26.mid_ref = bf16[16,16,128]{2,1,0:T(8,128)(2,1)S(1)} all-to-all(bf16[16,16,128]{2,1,0:T(8,128)(2,1)S(1)} %get-tuple-element.17), channel_id=1, replica_groups=mesh['x'=4,'y'=2,'core'=2,'mp'=32] {'x','y','core'}, dimensions={0} | all-to-all | bytes 131072 | tf_op jit(solution)/shard_map/all_to_all | solution.py:18
  76.5 0.6 shard_map.147
  77.1 17.1 %all_to_all.27 = bf16[32,8,128]{2,1,0:T(8,128)(2,1)S(1)} all-to-all(bf16[32,8,128]{2,1,0:T(8,128)(2,1)S(1)} %bitcast.13), channel_id=1, replica_groups=mesh['x'=4,'y'=2,'core'=2,'mp'=32] {'mp'}, dimensions={0} | all-to-all | bytes 131072 | tf_op jit(solution)/shard_map/all_to_all | solution.py:18
  94.2 0.8 shard_map.148
  (13 shorter events, 0.0 us)
Async XLA Ops:
  0.6 11.5 %copy-start.2 = (bf16[1,32,16,512]{3,2,1,0:T(8,128)(2,1)S(1)}, bf16[1,32,16,512]{3,2,1,0:T(8,128)(2,1)}, u32[]{:S(2)}) copy-start(bf16[1,32,16,512]{3,2,1,0:T(8,128)(2,1)} %up_ref.1) | copy-start | bytes 1572868
  0.6 11.5 %copy-start.3 = (bf16[1,32,16,512]{3,2,1,0:T(8,128)(2,1)S(1)}, bf16[1,32,16,512]{3,2,1,0:T(8,128)(2,1)}, u32[]{:S(2)}) copy-start(bf16[1,32,16,512]{3,2,1,0:T(8,128)(2,1)} %down_ref.1) | copy-start | bytes 1572868
  1.9 10.3 %collective-permute-start = (bf16[32,16,512]{2,1,0:T(8,128)(2,1)S(1)}, bf16[32,16,512]{2,1,0:T(8,128)(2,1)S(1)}, u32[]{:S(2)}, u32[]{:S(2)}) collective-permute-start(bf16[32,16,512]{2,1,0:T(8,128)(2,1)S(1)} %select_bitcast_fusion), channel_id=1, source_target_pairs={{0,32},{32,0},{1,33},{33,1},{2,34},{34,2},{3,35},{35,3},{4,36},{36... | collective-permute-start | bytes 1572872 | tf_op jit(solution)/shard_map/ppermute | solution.py:143
  13.1 27.3 %copy-start.1 = (bf16[1,512,512]{2,1,0:T(8,128)(2,1)S(1)}, bf16[1,512,512]{2,1,0:T(8,128)(2,1)}, u32[]{:S(2)}) copy-start(bf16[1,512,512]{2,1,0:T(8,128)(2,1)} %down_left.1) | copy-start | bytes 1572868
  13.1 12.8 %all-to-all-start = ((bf16[8,16,16,128]{3,2,1,0:T(8,128)(2,1)}), bf16[8,16,16,128]{3,2,1,0:T(8,128)(2,1)S(1)}, u32[]{:S(2)}, u32[]{:S(2)}) async-start(bf16[8,16,16,128]{3,2,1,0:T(8,128)(2,1)} %shard_map.145), calls=%async_computation | async-start | bytes 1048576 | tf_op jit(solution)/shard_map/all_to_all | solution.py:18
  16.8 23.6 %copy-start = (bf16[1,512,512]{2,1,0:T(8,128)(2,1)S(1)}, bf16[1,512,512]{2,1,0:T(8,128)(2,1)}, u32[]{:S(2)}) copy-start(bf16[1,512,512]{2,1,0:T(8,128)(2,1)} %up_left.1) | copy-start | bytes 1572868
  26.6 27.9 %all-to-all-start.1 = ((bf16[32,8,128]{2,1,0:T(8,128)(2,1)}), bf16[32,8,128]{2,1,0:T(8,128)(2,1)S(1)}, u32[]{:S(2)}, u32[]{:S(2)}) async-start(bf16[32,8,128]{2,1,0:T(8,128)(2,1)} %bitcast.3), calls=%async_computation.1 | async-start | bytes 131072 | tf_op jit(solution)/shard_map/all_to_all | solution.py:18
  40.4 25.9 %copy-start.5 = (bf16[1,512,512]{2,1,0:T(8,128)(2,1)S(1)}, bf16[1,512,512]{2,1,0:T(8,128)(2,1)}, u32[]{:S(2)}) copy-start(bf16[1,512,512]{2,1,0:T(8,128)(2,1)} %down_right.1) | copy-start | bytes 1572868
  40.4 25.9 %copy-start.9 = (f32[1,32,512]{2,1,0:T(8,128)S(1)}, f32[1,32,512]{2,1,0:T(8,128)}, u32[]{:S(2)}) copy-start(f32[1,32,512]{2,1,0:T(8,128)} %down_second.1) | copy-start | bytes 196612
  40.5 25.9 %copy-start.4 = (bf16[1,512,512]{2,1,0:T(8,128)(2,1)S(1)}, bf16[1,512,512]{2,1,0:T(8,128)(2,1)}, u32[]{:S(2)}) copy-start(bf16[1,512,512]{2,1,0:T(8,128)(2,1)} %up_right.1) | copy-start | bytes 1572868
  54.7 11.6 %copy-start.6 = (f32[1,32,512]{2,1,0:T(8,128)S(1)}, f32[1,32,512]{2,1,0:T(8,128)}, u32[]{:S(2)}) copy-start(f32[1,32,512]{2,1,0:T(8,128)} %up_first.1) | copy-start | bytes 196612
  54.8 11.6 %copy-start.7 = (f32[1,32,512]{2,1,0:T(8,128)S(1)}, f32[1,32,512]{2,1,0:T(8,128)}, u32[]{:S(2)}) copy-start(f32[1,32,512]{2,1,0:T(8,128)} %up_second.1) | copy-start | bytes 196612
  54.8 11.6 %copy-start.8 = (f32[1,32,512]{2,1,0:T(8,128)S(1)}, f32[1,32,512]{2,1,0:T(8,128)}, u32[]{:S(2)}) copy-start(f32[1,32,512]{2,1,0:T(8,128)} %down_first.1) | copy-start | bytes 196612

commit v3 on v2

--- a/solution.py
+++ b/solution.py
@@ -141,6 +141,9 @@
 
     sent = jnp.where(core == 0, down_partials[0], up_partials[0])
     got = lax.ppermute(sent, "core", [(0, 1), (1, 0)])
+    left = jnp.where(core == 0, up_left[0], down_left[0]).reshape(32, 2, 8, 512)
+    left = lax.dynamic_index_in_dim(left, part, 1, keepdims=False).reshape(256, 512)
+    got, left = lax.optimization_barrier((got, left))
     chunks = call(
         chunk_kernel,
         jax.ShapeDtypeStruct((8, 16, 16, 128), BF),
@@ -150,9 +153,6 @@
     )
     summed = jnp.sum(exchange(chunks, ("x", "y")).astype(F32), axis=0).astype(BF)
     grad = exchange(summed.reshape(32, 8, 128), "mp").reshape(256, 128)
-
-    left = jnp.where(core == 0, up_left[0], down_left[0]).reshape(32, 2, 8, 512)
-    left = lax.dynamic_index_in_dim(left, part, 1, keepdims=False).reshape(256, 512)
     half = jnp.einsum("pr,pq->rq", left, grad, preferred_element_type=F32)
     half = exchange(half.astype(BF).reshape(16, 32, 128), DP)
 

time: 95.4 us -> 93.7 us (0.982)
  blocking collectives: 37.4 us -> 77.7 us
  waiting for transfers between devices: 24.6 us -> 1.37 us
  starting transfers between devices: 26.2 us -> 8.78 us
    all_to_all x3 -> x5, blocking collectives: 37.4 us -> 77.7 us  [exchange(): return lax.all_to_all(x, axis, 0, 0, tiled=True)]
    all_to_all x2 -> x0, waiting for transfers between devices: 23.1 us -> none  [exchange(): return lax.all_to_all(x, axis, 0, 0, tiled=True)]
    all_to_all x2 -> x0, starting transfers between devices: 17.4 us -> none  [exchange(): return lax.all_to_all(x, axis, 0, 0, tiled=True)]
  transfers between devices with their start and end apart: 3 -> 1, of which waited for: 3 -> 1; matrix products, arithmetic and copies ran while one was open for 0% -> 0% of each run, Pallas kernels for 0% -> 0%
where the time goes in v3:
time: 93.7 us; the launch traced here: 93.3 us
  blocking collectives  77.7 us (83%)
  starting transfers between devices  8.78 us (9%)
  Pallas kernels  2.98 us (3%)
  waiting for transfers between devices  1.37 us (1%)
  other arithmetic  1.33 us (1%)
    all_to_all x5, blocking collectives, exchange(): return lax.all_to_all(x, axis, 0, 0, tiled=True)  77.7 us
    ppermute x1, starting transfers between devices, per_device(): got = lax.ppermute(sent, 'core', [(0, 1), (1, 0)])  8.78 us
    pallas_call x4, Pallas kernels, call(): pl.pallas_call(kernel, out_shape=out_shape, compiler_params=PARAMS)(*args)  2.98 us
  transfers between devices with their start and end apart: 1, of which 1 were waited for; matrix products, arithmetic and copies ran while one was open for 0% of the time, Pallas kernels for 0%

profile of v3, /device:TPU:1, one launch (start us, length us, event | category | flops | bytes accessed | tf_op | source)
XLA Modules:
  0.0 93.3 jit_solution(474245866026853278)
XLA Ops:
  0.7 1.2 %select_bitcast_fusion = bf16[32,16,512]{2,1,0:T(8,128)(2,1)S(1)} fusion(bf16[1,32,16,512]{3,2,1,0:T(8,128)(2,1)} %down_ref.1, bf16[1,32,16,512]{3,2,1,0:T(8,128)(2,1)} %up_ref.1, pred[]{:T(512)S(6)} %eq.4), kind=kLoop, calls=%fused_computation.1 | loop fusion | flops 262144 | bytes 1572865 | tf_op jit(solution)/shard_map/jit(_where)/select_n | solution.py:142
  1.9 8.8 %collective-permute-start = (bf16[32,16,512]{2,1,0:T(8,128)(2,1)S(1)}, bf16[32,16,512]{2,1,0:T(8,128)(2,1)S(1)}, u32[]{:S(2)}, u32[]{:S(2)}) collective-permute-start(bf16[32,16,512]{2,1,0:T(8,128)(2,1)S(1)} %select_bitcast_fusion), channel_id=1, source_target_pairs={{0,32},{32,0},{1,33},{33,1},{2,34},{34,2},{3,35},{35,3},{4,36},{36... | collective-permute-start | bytes 1572872 | tf_op jit(solution)/shard_map/ppermute | solution.py:143
  10.7 0.0 copy-start.3
  10.7 0.1 broadcast_select_fusion
  10.8 0.0 copy-start.2
  10.8 1.4 %collective-permute-done.got_ref = bf16[32,16,512]{2,1,0:T(8,128)(2,1)S(1)} collective-permute-done((bf16[32,16,512]{2,1,0:T(8,128)(2,1)S(1)}, bf16[32,16,512]{2,1,0:T(8,128)(2,1)S(1)}, u32[]{:S(2)}, u32[]{:S(2)}) %collective-permute-start) | collective-permute-done | bytes 524320 | tf_op jit(solution)/shard_map/ppermute | solution.py:143
  12.2 0.2 shard_map.145
  12.3 11.7 %all_to_all.25 = bf16[8,16,16,128]{3,2,1,0:T(8,128)(2,1)S(1)} all-to-all(bf16[8,16,16,128]{3,2,1,0:T(8,128)(2,1)S(1)} %shard_map.145), channel_id=1, replica_groups=mesh['x'=4,'y'=2,'core'=2,'mp'=32] {'x','y'}, dimensions={0} | all-to-all | bytes 1048576 | tf_op jit(solution)/shard_map/all_to_all | solution.py:18
  24.1 0.1 reduce_sum.12
  24.2 0.0 copy-start.4
  24.2 27.9 %all_to_all.26 = bf16[32,8,128]{2,1,0:T(8,128)(2,1)S(1)} all-to-all(bf16[32,8,128]{2,1,0:T(8,128)(2,1)S(1)} %bitcast.17), channel_id=1, replica_groups=mesh['x'=4,'y'=2,'core'=2,'mp'=32] {'mp'}, dimensions={0} | all-to-all | bytes 131072 | tf_op jit(solution)/shard_map/all_to_all | solution.py:18
  52.0 0.3 convolution_convert_fusion
  52.3 0.0 copy-start.6
  52.3 0.0 copy-start.7
  52.3 0.0 copy-start.8
  52.3 0.0 copy-start.9
  52.4 12.4 %all_to_all.27.half_ref = bf16[16,32,128]{2,1,0:T(8,128)(2,1)S(1)} all-to-all(bf16[16,32,128]{2,1,0:T(8,128)(2,1)S(1)} %bitcast.16), channel_id=1, replica_groups=mesh['x'=4,'y'=2,'core'=2,'mp'=32] {'x','y','core'}, dimensions={0} | all-to-all | bytes 262144 | tf_op jit(solution)/shard_map/all_to_all | solution.py:18
  64.8 0.0 copy-done.6
  64.8 0.0 copy-done.7
  64.8 1.4 %shard_map.146 = (f32[1,32,512]{2,1,0:T(8,128)}, f32[1,32,512]{2,1,0:T(8,128)}, f32[1,32,512]{2,1,0:T(8,128)}, f32[1,32,512]{2,1,0:T(8,128)}, bf16[16,16,128]{2,1,0:T(8,128)(2,1)S(1)}) custom-call(bf16[16,32,128]{2,1,0:T(8,128)(2,1)S(1)} %all_to_all.27.half_ref, bf16[1,512,512]{2,1,0:T(8,128)(2,1)S(1)} %copy-done.4, bf16[1,512,512]{2,1,0:T(8,128)(2,1)S(1)} %copy-done.5, ...), custom_call_target="tpu_custom_call" | custom-call | tf_op jit(solution)/shard_map/pallas_call | solution.py:22
  66.3 8.7 %all_to_all.28.mid_ref = bf16[16,16,128]{2,1,0:T(8,128)(2,1)S(1)} all-to-all(bf16[16,16,128]{2,1,0:T(8,128)(2,1)S(1)} %get-tuple-element.21), channel_id=1, replica_groups=mesh['x'=4,'y'=2,'core'=2,'mp'=32] {'x','y','core'}, dimensions={0} | all-to-all | bytes 131072 | tf_op jit(solution)/shard_map/all_to_all | solution.py:18
  75.0 0.6 shard_map.147
  75.5 17.0 %all_to_all.29 = bf16[32,8,128]{2,1,0:T(8,128)(2,1)S(1)} all-to-all(bf16[32,8,128]{2,1,0:T(8,128)(2,1)S(1)} %bitcast.13), channel_id=1, replica_groups=mesh['x'=4,'y'=2,'core'=2,'mp'=32] {'mp'}, dimensions={0} | all-to-all | bytes 131072 | tf_op jit(solution)/shard_map/all_to_all | solution.py:18
  92.5 0.8 shard_map.148
  (12 shorter events, 0.0 us)
Async XLA Ops:
  0.6 10.0 %copy-start = (bf16[1,512,512]{2,1,0:T(8,128)(2,1)S(1)}, bf16[1,512,512]{2,1,0:T(8,128)(2,1)}, u32[]{:S(2)}) copy-start(bf16[1,512,512]{2,1,0:T(8,128)(2,1)} %up_left.1) | copy-start | bytes 1572868
  0.6 10.0 %copy-start.1 = (bf16[1,512,512]{2,1,0:T(8,128)(2,1)S(1)}, bf16[1,512,512]{2,1,0:T(8,128)(2,1)}, u32[]{:S(2)}) copy-start(bf16[1,512,512]{2,1,0:T(8,128)(2,1)} %down_left.1) | copy-start | bytes 1572868
  1.9 10.3 %collective-permute-start = (bf16[32,16,512]{2,1,0:T(8,128)(2,1)S(1)}, bf16[32,16,512]{2,1,0:T(8,128)(2,1)S(1)}, u32[]{:S(2)}, u32[]{:S(2)}) collective-permute-start(bf16[32,16,512]{2,1,0:T(8,128)(2,1)S(1)} %select_bitcast_fusion), channel_id=1, source_target_pairs={{0,32},{32,0},{1,33},{33,1},{2,34},{34,2},{3,35},{35,3},{4,36},{36... | collective-permute-start | bytes 1572872 | tf_op jit(solution)/shard_map/ppermute | solution.py:143
  10.7 1.5 %copy-start.3 = (bf16[1,32,16,512]{3,2,1,0:T(8,128)(2,1)S(1)}, bf16[1,32,16,512]{3,2,1,0:T(8,128)(2,1)}, u32[]{:S(2)}) copy-start(bf16[1,32,16,512]{3,2,1,0:T(8,128)(2,1)} %down_ref.1) | copy-start | bytes 1572868
  10.8 1.4 %copy-start.2 = (bf16[1,32,16,512]{3,2,1,0:T(8,128)(2,1)S(1)}, bf16[1,32,16,512]{3,2,1,0:T(8,128)(2,1)}, u32[]{:S(2)}) copy-start(bf16[1,32,16,512]{3,2,1,0:T(8,128)(2,1)} %up_ref.1) | copy-start | bytes 1572868
  24.1 40.7 %copy-start.5 = (bf16[1,512,512]{2,1,0:T(8,128)(2,1)S(1)}, bf16[1,512,512]{2,1,0:T(8,128)(2,1)}, u32[]{:S(2)}) copy-start(bf16[1,512,512]{2,1,0:T(8,128)(2,1)} %down_right.1) | copy-start | bytes 1572868
  24.2 40.6 %copy-start.4 = (bf16[1,512,512]{2,1,0:T(8,128)(2,1)S(1)}, bf16[1,512,512]{2,1,0:T(8,128)(2,1)}, u32[]{:S(2)}) copy-start(bf16[1,512,512]{2,1,0:T(8,128)(2,1)} %up_right.1) | copy-start | bytes 1572868
  52.3 12.5 %copy-start.6 = (f32[1,32,512]{2,1,0:T(8,128)S(1)}, f32[1,32,512]{2,1,0:T(8,128)}, u32[]{:S(2)}) copy-start(f32[1,32,512]{2,1,0:T(8,128)} %up_first.1) | copy-start | bytes 196612
  52.3 12.5 %copy-start.7 = (f32[1,32,512]{2,1,0:T(8,128)S(1)}, f32[1,32,512]{2,1,0:T(8,128)}, u32[]{:S(2)}) copy-start(f32[1,32,512]{2,1,0:T(8,128)} %up_second.1) | copy-start | bytes 196612
  52.3 12.5 %copy-start.8 = (f32[1,32,512]{2,1,0:T(8,128)S(1)}, f32[1,32,512]{2,1,0:T(8,128)}, u32[]{:S(2)}) copy-start(f32[1,32,512]{2,1,0:T(8,128)} %down_first.1) | copy-start | bytes 196612
  52.3 12.5 %copy-start.9 = (f32[1,32,512]{2,1,0:T(8,128)S(1)}, f32[1,32,512]{2,1,0:T(8,128)}, u32[]{:S(2)}) copy-start(f32[1,32,512]{2,1,0:T(8,128)} %down_second.1) | copy-start | bytes 196612

commit v4 on v3

--- a/solution.py
+++ b/solution.py
@@ -116,7 +116,10 @@
     out_ref[...] = jnp.where(lane < 64, top, low).reshape(16, 16, 128).astype(BF)
 
 
-def unpack_kernel(got_ref, up_ref, down_ref):
+def unpack_kernel(got_ref, *refs):
+    *moments, up_ref, down_ref = refs
+    for own_ref, out_ref in zip(moments[:4], moments[4:]):
+        out_ref[...] = own_ref[...]
     got = got_ref[...].astype(F32).reshape(256, 128)
     low = pltpu.roll(got, 64, 1)
     rows = jnp.stack([got.reshape(32, 8, 128), low.reshape(32, 8, 128)], axis=1)
@@ -173,8 +176,8 @@
         back_kernel, jax.ShapeDtypeStruct((16, 16, 128), BF), mid, up_left, down_left
     )
     packed = exchange(packed.reshape(32, 8, 128), "mp").reshape(16, 16, 128)
-    updates = call(unpack_kernel, [jax.ShapeDtypeStruct((32, 16, 32), BF)] * 2, packed)
-    return (*moments, *updates)
+    update = jax.ShapeDtypeStruct((32, 16, 32), BF)
+    return tuple(call(unpack_kernel, [rows] * 4 + [update] * 2, packed, *moments))
 
 
 def solution(mesh):

time: 93.7 us -> 93.2 us (level)
  no operation moved by 1% of the time
where the time goes in v4:
time: 93.2 us; the launch traced here: 92.8 us
  blocking collectives  77.7 us (83%)
  starting transfers between devices  8.78 us (9%)
  Pallas kernels  2.45 us (3%)
  waiting for transfers between devices  1.37 us (1%)
  other arithmetic  1.33 us (1%)
    all_to_all x5, blocking collectives, exchange(): return lax.all_to_all(x, axis, 0, 0, tiled=True)  77.7 us
    ppermute x1, starting transfers between devices, per_device(): got = lax.ppermute(sent, 'core', [(0, 1), (1, 0)])  8.78 us
    pallas_call x4, Pallas kernels, call(): pl.pallas_call(kernel, out_shape=out_shape, compiler_params=PARAMS)(*args)  2.45 us
  transfers between devices with their start and end apart: 1, of which 1 were waited for; matrix products, arithmetic and copies ran while one was open for 0% of the time, Pallas kernels for 0%

profile of v4, /device:TPU:1, one launch (start us, length us, event | category | flops | bytes accessed | tf_op | source)
XLA Modules:
  0.0 92.8 jit_solution(6172569805568569068)
XLA Ops:
  0.7 1.2 %select_bitcast_fusion = bf16[32,16,512]{2,1,0:T(8,128)(2,1)S(1)} fusion(bf16[1,32,16,512]{3,2,1,0:T(8,128)(2,1)} %down_ref.1, bf16[1,32,16,512]{3,2,1,0:T(8,128)(2,1)} %up_ref.1, pred[]{:T(512)S(6)} %eq.4), kind=kLoop, calls=%fused_computation.1 | loop fusion | flops 262144 | bytes 1572865 | tf_op jit(solution)/shard_map/jit(_where)/select_n | solution.py:145
  1.9 8.8 %collective-permute-start = (bf16[32,16,512]{2,1,0:T(8,128)(2,1)S(1)}, bf16[32,16,512]{2,1,0:T(8,128)(2,1)S(1)}, u32[]{:S(2)}, u32[]{:S(2)}) collective-permute-start(bf16[32,16,512]{2,1,0:T(8,128)(2,1)S(1)} %select_bitcast_fusion), channel_id=1, source_target_pairs={{0,32},{32,0},{1,33},{33,1},{2,34},{34,2},{3,35},{35,3},{4,36},{36... | collective-permute-start | bytes 1572872 | tf_op jit(solution)/shard_map/ppermute | solution.py:146
  10.7 0.0 copy-start.3
  10.7 0.1 broadcast_select_fusion
  10.8 0.0 copy-start.2
  10.8 1.4 %collective-permute-done.got_ref = bf16[32,16,512]{2,1,0:T(8,128)(2,1)S(1)} collective-permute-done((bf16[32,16,512]{2,1,0:T(8,128)(2,1)S(1)}, bf16[32,16,512]{2,1,0:T(8,128)(2,1)S(1)}, u32[]{:S(2)}, u32[]{:S(2)}) %collective-permute-start) | collective-permute-done | bytes 524320 | tf_op jit(solution)/shard_map/ppermute | solution.py:146
  12.2 0.2 shard_map.145
  12.3 11.7 %all_to_all.25 = bf16[8,16,16,128]{3,2,1,0:T(8,128)(2,1)S(1)} all-to-all(bf16[8,16,16,128]{3,2,1,0:T(8,128)(2,1)S(1)} %shard_map.145), channel_id=1, replica_groups=mesh['x'=4,'y'=2,'core'=2,'mp'=32] {'x','y'}, dimensions={0} | all-to-all | bytes 1048576 | tf_op jit(solution)/shard_map/all_to_all | solution.py:18
  24.1 0.1 reduce_sum.12
  24.2 0.0 copy-start.4
  24.2 27.9 %all_to_all.26 = bf16[32,8,128]{2,1,0:T(8,128)(2,1)S(1)} all-to-all(bf16[32,8,128]{2,1,0:T(8,128)(2,1)S(1)} %bitcast.17), channel_id=1, replica_groups=mesh['x'=4,'y'=2,'core'=2,'mp'=32] {'mp'}, dimensions={0} | all-to-all | bytes 131072 | tf_op jit(solution)/shard_map/all_to_all | solution.py:18
  52.0 0.3 convolution_convert_fusion
  52.3 0.0 copy-start.6
  52.3 0.0 copy-start.7
  52.3 0.0 copy-start.8
  52.3 0.0 copy-start.9
  52.4 12.4 %all_to_all.27.half_ref = bf16[16,32,128]{2,1,0:T(8,128)(2,1)S(1)} all-to-all(bf16[16,32,128]{2,1,0:T(8,128)(2,1)S(1)} %bitcast.16), channel_id=1, replica_groups=mesh['x'=4,'y'=2,'core'=2,'mp'=32] {'x','y','core'}, dimensions={0} | all-to-all | bytes 262144 | tf_op jit(solution)/shard_map/all_to_all | solution.py:18
  64.8 0.0 copy-done.6
  64.8 0.0 copy-done.7
  64.8 0.8 shard_map.146
  65.7 8.7 %all_to_all.28.mid_ref = bf16[16,16,128]{2,1,0:T(8,128)(2,1)S(1)} all-to-all(bf16[16,16,128]{2,1,0:T(8,128)(2,1)S(1)} %get-tuple-element.15), channel_id=1, replica_groups=mesh['x'=4,'y'=2,'core'=2,'mp'=32] {'x','y','core'}, dimensions={0} | all-to-all | bytes 131072 | tf_op jit(solution)/shard_map/all_to_all | solution.py:18
  74.4 0.6 shard_map.147
  75.0 17.0 %all_to_all.29 = bf16[32,8,128]{2,1,0:T(8,128)(2,1)S(1)} all-to-all(bf16[32,8,128]{2,1,0:T(8,128)(2,1)S(1)} %bitcast.14), channel_id=1, replica_groups=mesh['x'=4,'y'=2,'core'=2,'mp'=32] {'mp'}, dimensions={0} | all-to-all | bytes 131072 | tf_op jit(solution)/shard_map/all_to_all | solution.py:18
  91.9 0.9 shard_map.148
  (12 shorter events, 0.0 us)
Async XLA Ops:
  0.6 10.0 %copy-start = (bf16[1,512,512]{2,1,0:T(8,128)(2,1)S(1)}, bf16[1,512,512]{2,1,0:T(8,128)(2,1)}, u32[]{:S(2)}) copy-start(bf16[1,512,512]{2,1,0:T(8,128)(2,1)} %up_left.1) | copy-start | bytes 1572868
  0.6 10.0 %copy-start.1 = (bf16[1,512,512]{2,1,0:T(8,128)(2,1)S(1)}, bf16[1,512,512]{2,1,0:T(8,128)(2,1)}, u32[]{:S(2)}) copy-start(bf16[1,512,512]{2,1,0:T(8,128)(2,1)} %down_left.1) | copy-start | bytes 1572868
  1.9 10.3 %collective-permute-start = (bf16[32,16,512]{2,1,0:T(8,128)(2,1)S(1)}, bf16[32,16,512]{2,1,0:T(8,128)(2,1)S(1)}, u32[]{:S(2)}, u32[]{:S(2)}) collective-permute-start(bf16[32,16,512]{2,1,0:T(8,128)(2,1)S(1)} %select_bitcast_fusion), channel_id=1, source_target_pairs={{0,32},{32,0},{1,33},{33,1},{2,34},{34,2},{3,35},{35,3},{4,36},{36... | collective-permute-start | bytes 1572872 | tf_op jit(solution)/shard_map/ppermute | solution.py:146
  10.7 1.5 %copy-start.3 = (bf16[1,32,16,512]{3,2,1,0:T(8,128)(2,1)S(1)}, bf16[1,32,16,512]{3,2,1,0:T(8,128)(2,1)}, u32[]{:S(2)}) copy-start(bf16[1,32,16,512]{3,2,1,0:T(8,128)(2,1)} %down_ref.1) | copy-start | bytes 1572868
  10.8 1.4 %copy-start.2 = (bf16[1,32,16,512]{3,2,1,0:T(8,128)(2,1)S(1)}, bf16[1,32,16,512]{3,2,1,0:T(8,128)(2,1)}, u32[]{:S(2)}) copy-start(bf16[1,32,16,512]{3,2,1,0:T(8,128)(2,1)} %up_ref.1) | copy-start | bytes 1572868
  24.1 40.7 %copy-start.5 = (bf16[1,512,512]{2,1,0:T(8,128)(2,1)S(1)}, bf16[1,512,512]{2,1,0:T(8,128)(2,1)}, u32[]{:S(2)}) copy-start(bf16[1,512,512]{2,1,0:T(8,128)(2,1)} %down_right.1) | copy-start | bytes 1572868
  24.2 40.6 %copy-start.4 = (bf16[1,512,512]{2,1,0:T(8,128)(2,1)S(1)}, bf16[1,512,512]{2,1,0:T(8,128)(2,1)}, u32[]{:S(2)}) copy-start(bf16[1,512,512]{2,1,0:T(8,128)(2,1)} %up_right.1) | copy-start | bytes 1572868
  52.3 12.5 %copy-start.6 = (f32[1,32,512]{2,1,0:T(8,128)S(1)}, f32[1,32,512]{2,1,0:T(8,128)}, u32[]{:S(2)}) copy-start(f32[1,32,512]{2,1,0:T(8,128)} %up_first.1) | copy-start | bytes 196612
  52.3 12.5 %copy-start.7 = (f32[1,32,512]{2,1,0:T(8,128)S(1)}, f32[1,32,512]{2,1,0:T(8,128)}, u32[]{:S(2)}) copy-start(f32[1,32,512]{2,1,0:T(8,128)} %up_second.1) | copy-start | bytes 196612
  52.3 12.5 %copy-start.8 = (f32[1,32,512]{2,1,0:T(8,128)S(1)}, f32[1,32,512]{2,1,0:T(8,128)}, u32[]{:S(2)}) copy-start(f32[1,32,512]{2,1,0:T(8,128)} %down_first.1) | copy-start | bytes 196612
  52.3 12.5 %copy-start.9 = (f32[1,32,512]{2,1,0:T(8,128)S(1)}, f32[1,32,512]{2,1,0:T(8,128)}, u32[]{:S(2)}) copy-start(f32[1,32,512]{2,1,0:T(8,128)} %down_second.1) | copy-start | bytes 196612

commit v5 on v4

--- a/solution.py
+++ b/solution.py
@@ -11,6 +11,7 @@
 BF = jnp.bfloat16
 F32 = jnp.float32
 DP = ("x", "y", "core")
+MP = ("z", "h")
 PARAMS = pltpu.CompilerParams(vmem_limit_bytes=16 * 2**20)
 
 
@@ -29,7 +30,9 @@
             total = own_ref[0, :, :, lanes].astype(F32) + got_ref[:, :, lanes].astype(F32)
             total = total.reshape(16, 2, 2, 8, 128)
             for half in range(2):
-                out_ref[2 * at + half] = total[:, :, half].reshape(16, 16, 128).astype(BF)
+                for odd in range(2):
+                    part = total[:, odd, half].reshape(8, 16, 128)
+                    out_ref[8 * odd + 2 * at + 1 * half] = part.astype(BF)
 
     core = lax.axis_index("core")
 
@@ -40,6 +43,17 @@
     @pl.when(core == 1)
     def _():
         chunks(down_ref)
+
+
+def sum_kernel(got_ref, out_ref):
+    sums = []
+    for odd in range(2):
+        total = 0.0
+        for at in range(4):
+            for half in range(2):
+                total = total + got_ref[8 * odd + 2 * at + 1 * half].astype(F32)
+        sums.append(total.reshape(16, 8, 128))
+    out_ref[...] = jnp.stack(sums, axis=1).reshape(16, 16, 128).astype(BF)
 
 
 def middle_kernel(
@@ -149,13 +163,14 @@
     got, left = lax.optimization_barrier((got, left))
     chunks = call(
         chunk_kernel,
-        jax.ShapeDtypeStruct((8, 16, 16, 128), BF),
+        jax.ShapeDtypeStruct((16, 8, 16, 128), BF),
         up_partials,
         down_partials,
         got,
     )
-    summed = jnp.sum(exchange(chunks, ("x", "y")).astype(F32), axis=0).astype(BF)
-    grad = exchange(summed.reshape(32, 8, 128), "mp").reshape(256, 128)
+    got = exchange(chunks, ("h", "x", "y"))
+    summed = call(sum_kernel, jax.ShapeDtypeStruct((16, 16, 128), BF), got)
+    grad = exchange(summed, "z").reshape(256, 128)
     half = jnp.einsum("pr,pq->rq", left, grad, preferred_element_type=F32)
     half = exchange(half.astype(BF).reshape(16, 32, 128), DP)
 
@@ -175,15 +190,15 @@
     packed = call(
         back_kernel, jax.ShapeDtypeStruct((16, 16, 128), BF), mid, up_left, down_left
     )
-    packed = exchange(packed.reshape(32, 8, 128), "mp").reshape(16, 16, 128)
+    packed = exchange(packed.reshape(32, 8, 128), ("z", "h")).reshape(16, 16, 128)
     update = jax.ShapeDtypeStruct((32, 16, 32), BF)
     return tuple(call(unpack_kernel, [rows] * 4 + [update] * 2, packed, *moments))
 
 
 def solution(mesh):
-    mesh = Mesh(mesh.devices.reshape(4, 2, 2, 32), ("x", "y", "core", "mp"))
-    blocks, rows = P("mp", None, None), P("mp", DP, None)
-    partials, update = P(DP, None, "mp", None), P(None, "mp", DP)
+    mesh = Mesh(mesh.devices.reshape(4, 2, 2, 16, 2), ("x", "y", "core", "z", "h"))
+    blocks, rows = P(MP, None, None), P(MP, DP, None)
+    partials, update = P(DP, None, MP, None), P(None, MP, DP)
     return jax.shard_map(
         per_device,
         mesh=mesh,

time: 93.2 us -> 92.3 us (level)
    pallas_call x4 -> x5, Pallas kernels: 2.45 us -> 2.52 us  [call(): pl.pallas_call(kernel, out_shape=out_shape, compiler_params=PARAMS)(*args)]
where the time goes in v5:
time: 92.3 us; the launch traced here: 91.9 us
  blocking collectives  76.8 us (83%)
  starting transfers between devices  8.78 us (10%)
  Pallas kernels  2.52 us (3%)
  waiting for transfers between devices  1.37 us (1%)
  other arithmetic  1.25 us (1%)
    all_to_all x5, blocking collectives, exchange(): return lax.all_to_all(x, axis, 0, 0, tiled=True)  76.8 us
    ppermute x1, starting transfers between devices, per_device(): got = lax.ppermute(sent, 'core', [(0, 1), (1, 0)])  8.78 us
    pallas_call x5, Pallas kernels, call(): pl.pallas_call(kernel, out_shape=out_shape, compiler_params=PARAMS)(*args)  2.52 us
  transfers between devices with their start and end apart: 1, of which 1 were waited for; matrix products, arithmetic and copies ran while one was open for 0% of the time, Pallas kernels for 0%

profile of v5, /device:TPU:1, one launch (start us, length us, event | category | flops | bytes accessed | tf_op | source)
XLA Modules:
  0.0 91.9 jit_solution(12913547982928489544)
XLA Ops:
  0.6 0.0 copy-start
  0.7 1.2 %select_bitcast_fusion = bf16[32,16,512]{2,1,0:T(8,128)(2,1)S(1)} fusion(bf16[1,32,16,512]{3,2,1,0:T(8,128)(2,1)} %down_ref.1, bf16[1,32,16,512]{3,2,1,0:T(8,128)(2,1)} %up_ref.1, pred[]{:T(512)S(6)} %eq.4), kind=kLoop, calls=%fused_computation.1 | loop fusion | flops 262144 | bytes 1572865 | tf_op jit(solution)/shard_map/jit(_where)/select_n | solution.py:159
  1.9 8.8 %collective-permute-start = (bf16[32,16,512]{2,1,0:T(8,128)(2,1)S(1)}, bf16[32,16,512]{2,1,0:T(8,128)(2,1)S(1)}, u32[]{:S(2)}, u32[]{:S(2)}) collective-permute-start(bf16[32,16,512]{2,1,0:T(8,128)(2,1)S(1)} %select_bitcast_fusion), channel_id=1, source_target_pairs={{0,32},{32,0},{1,33},{33,1},{2,34},{34,2},{3,35},{35,3},{4,36},{36... | collective-permute-start | bytes 1572872 | tf_op jit(solution)/shard_map/ppermute | solution.py:160
  10.7 0.0 copy-start.3
  10.7 0.1 broadcast_select_fusion
  10.8 0.0 copy-start.2
  10.8 1.4 %collective-permute-done.got_ref = bf16[32,16,512]{2,1,0:T(8,128)(2,1)S(1)} collective-permute-done((bf16[32,16,512]{2,1,0:T(8,128)(2,1)S(1)}, bf16[32,16,512]{2,1,0:T(8,128)(2,1)S(1)}, u32[]{:S(2)}, u32[]{:S(2)}) %collective-permute-start) | collective-permute-done | bytes 524320 | tf_op jit(solution)/shard_map/ppermute | solution.py:160
  12.2 0.2 shard_map.145
  12.3 13.6 %all_to_all.25.got_ref = bf16[16,8,16,128]{3,2,1,0:T(8,128)(2,1)S(1)} all-to-all(bf16[16,8,16,128]{3,2,1,0:T(8,128)(2,1)S(1)} %shard_map.145), channel_id=1, replica_groups=mesh['x'=4,'y'=2,'core'=2,'z'=16,'h'=2] {'h','x','y'}, dimensions={0} | all-to-all | bytes 1048576 | tf_op jit(solution)/shard_map/all_to_all | solution.py:19
  26.0 0.1 shard_map.146
  26.1 0.0 copy-start.4
  26.1 24.7 %all_to_all.26 = bf16[16,16,128]{2,1,0:T(8,128)(2,1)S(1)} all-to-all(bf16[16,16,128]{2,1,0:T(8,128)(2,1)S(1)} %shard_map.146), channel_id=1, replica_groups=mesh['x'=4,'y'=2,'core'=2,'z'=16,'h'=2] {'z'}, dimensions={0} | all-to-all | bytes 131072 | tf_op jit(solution)/shard_map/all_to_all | solution.py:19
  50.7 0.3 convolution_convert_fusion
  51.0 0.0 copy-start.6
  51.0 0.0 copy-start.7
  51.0 0.0 copy-start.8
  51.0 0.0 copy-start.9
  51.0 12.0 %all_to_all.27.half_ref = bf16[16,32,128]{2,1,0:T(8,128)(2,1)S(1)} all-to-all(bf16[16,32,128]{2,1,0:T(8,128)(2,1)S(1)} %bitcast.14), channel_id=1, replica_groups=mesh['x'=4,'y'=2,'core'=2,'z'=16,'h'=2] {'x','y','core'}, dimensions={0} | all-to-all | bytes 262144 | tf_op jit(solution)/shard_map/all_to_all | solution.py:19
  63.1 0.0 copy-done.4
  63.1 0.8 shard_map.147
  63.9 8.8 %all_to_all.28.mid_ref = bf16[16,16,128]{2,1,0:T(8,128)(2,1)S(1)} all-to-all(bf16[16,16,128]{2,1,0:T(8,128)(2,1)S(1)} %get-tuple-element.15), channel_id=1, replica_groups=mesh['x'=4,'y'=2,'core'=2,'z'=16,'h'=2] {'x','y','core'}, dimensions={0} | all-to-all | bytes 131072 | tf_op jit(solution)/shard_map/all_to_all | solution.py:19
  72.7 0.6 shard_map.148
  73.3 17.7 %all_to_all.29 = bf16[32,8,128]{2,1,0:T(8,128)(2,1)S(1)} all-to-all(bf16[32,8,128]{2,1,0:T(8,128)(2,1)S(1)} %bitcast.12), channel_id=1, replica_groups=mesh['x'=4,'y'=2,'core'=2,'z'=16,'h'=2] {'z','h'}, dimensions={0} | all-to-all | bytes 131072 | tf_op jit(solution)/shard_map/all_to_all | solution.py:19
  91.0 0.9 shard_map.149
  (12 shorter events, 0.0 us)
Async XLA Ops:
  0.6 10.0 %copy-start = (bf16[1,512,512]{2,1,0:T(8,128)(2,1)S(1)}, bf16[1,512,512]{2,1,0:T(8,128)(2,1)}, u32[]{:S(2)}) copy-start(bf16[1,512,512]{2,1,0:T(8,128)(2,1)} %up_left.1) | copy-start | bytes 1572868
  0.6 10.0 %copy-start.1 = (bf16[1,512,512]{2,1,0:T(8,128)(2,1)S(1)}, bf16[1,512,512]{2,1,0:T(8,128)(2,1)}, u32[]{:S(2)}) copy-start(bf16[1,512,512]{2,1,0:T(8,128)(2,1)} %down_left.1) | copy-start | bytes 1572868
  1.9 10.3 %collective-permute-start = (bf16[32,16,512]{2,1,0:T(8,128)(2,1)S(1)}, bf16[32,16,512]{2,1,0:T(8,128)(2,1)S(1)}, u32[]{:S(2)}, u32[]{:S(2)}) collective-permute-start(bf16[32,16,512]{2,1,0:T(8,128)(2,1)S(1)} %select_bitcast_fusion), channel_id=1, source_target_pairs={{0,32},{32,0},{1,33},{33,1},{2,34},{34,2},{3,35},{35,3},{4,36},{36... | collective-permute-start | bytes 1572872 | tf_op jit(solution)/shard_map/ppermute | solution.py:160
  10.7 1.5 %copy-start.3 = (bf16[1,32,16,512]{3,2,1,0:T(8,128)(2,1)S(1)}, bf16[1,32,16,512]{3,2,1,0:T(8,128)(2,1)}, u32[]{:S(2)}) copy-start(bf16[1,32,16,512]{3,2,1,0:T(8,128)(2,1)} %down_ref.1) | copy-start | bytes 1572868
  10.8 1.4 %copy-start.2 = (bf16[1,32,16,512]{3,2,1,0:T(8,128)(2,1)S(1)}, bf16[1,32,16,512]{3,2,1,0:T(8,128)(2,1)}, u32[]{:S(2)}) copy-start(bf16[1,32,16,512]{3,2,1,0:T(8,128)(2,1)} %up_ref.1) | copy-start | bytes 1572868
  26.0 37.1 %copy-start.5 = (bf16[1,512,512]{2,1,0:T(8,128)(2,1)S(1)}, bf16[1,512,512]{2,1,0:T(8,128)(2,1)}, u32[]{:S(2)}) copy-start(bf16[1,512,512]{2,1,0:T(8,128)(2,1)} %down_right.1) | copy-start | bytes 1572868
  26.1 37.0 %copy-start.4 = (bf16[1,512,512]{2,1,0:T(8,128)(2,1)S(1)}, bf16[1,512,512]{2,1,0:T(8,128)(2,1)}, u32[]{:S(2)}) copy-start(bf16[1,512,512]{2,1,0:T(8,128)(2,1)} %up_right.1) | copy-start | bytes 1572868
  51.0 12.1 %copy-start.6 = (f32[1,32,512]{2,1,0:T(8,128)S(1)}, f32[1,32,512]{2,1,0:T(8,128)}, u32[]{:S(2)}) copy-start(f32[1,32,512]{2,1,0:T(8,128)} %up_first.1) | copy-start | bytes 196612
  51.0 12.1 %copy-start.7 = (f32[1,32,512]{2,1,0:T(8,128)S(1)}, f32[1,32,512]{2,1,0:T(8,128)}, u32[]{:S(2)}) copy-start(f32[1,32,512]{2,1,0:T(8,128)} %up_second.1) | copy-start | bytes 196612
  51.0 12.1 %copy-start.8 = (f32[1,32,512]{2,1,0:T(8,128)S(1)}, f32[1,32,512]{2,1,0:T(8,128)}, u32[]{:S(2)}) copy-start(f32[1,32,512]{2,1,0:T(8,128)} %down_first.1) | copy-start | bytes 196612
  51.0 12.1 %copy-start.9 = (f32[1,32,512]{2,1,0:T(8,128)S(1)}, f32[1,32,512]{2,1,0:T(8,128)}, u32[]{:S(2)}) copy-start(f32[1,32,512]{2,1,0:T(8,128)} %down_second.1) | copy-start | bytes 196612

commit v6 on v5

--- a/solution.py
+++ b/solution.py
@@ -70,32 +70,36 @@
     down_second_new,
     mid_ref,
 ):
-    mids = []
-    for k, (right, first, second, first_out, second_out) in enumerate(
-        (
-            (up_right, up_first, up_second, up_first_new, up_second_new),
-            (down_right, down_first, down_second, down_first_new, down_second_new),
-        )
-    ):
+    sides = (
+        (up_right, up_first, up_second, up_first_new, up_second_new),
+        (down_right, down_first, down_second, down_first_new, down_second_new),
+    )
+    rotated = []
+    for k in range(2):
         tiles = [
             (half_ref[4 * at + k].astype(F32) + half_ref[4 * at + 2 + k].astype(F32)).astype(BF)
             for at in range(4)
         ]
         rows = jnp.concatenate(tiles, axis=1)
-        rotated = jnp.dot(rows, right[0], preferred_element_type=F32)
-        first_new = 0.9 * first[0] + 0.1 * rotated
-        second_new = 0.95 * second[0] + 0.05 * rotated * rotated
+        rotated.append(jnp.dot(rows, sides[k][0][0], preferred_element_type=F32))
+    directions = []
+    for k in range(2):
+        _, first, second, first_out, second_out = sides[k]
+        first_new = 0.9 * first[0] + 0.1 * rotated[k]
+        second_new = 0.95 * second[0] + 0.05 * rotated[k] * rotated[k]
         first_out[0] = first_new
         second_out[0] = second_new
         direction = first_new / CORR_FIRST / (jnp.sqrt(second_new / CORR_SECOND) + 1e-08)
-        mids.append(
-            lax.dot_general(
-                direction.astype(BF),
-                right[0],
-                (((1,), (1,)), ((), ())),
-                preferred_element_type=F32,
-            )
+        directions.append(direction.astype(BF))
+    mids = [
+        lax.dot_general(
+            directions[k],
+            sides[k][0][0],
+            (((1,), (1,)), ((), ())),
+            preferred_element_type=F32,
         )
+        for k in range(2)
+    ]
     lane = lax.broadcasted_iota(jnp.int32, (16, 128), 1)
     for at in range(4):
         pieces = [

time: 92.3 us -> 92.1 us (level)
  no operation moved by 1% of the time
where the time goes in v6:
time: 92.1 us; the launch traced here: 91.8 us
  blocking collectives  76.8 us (83%)
  starting transfers between devices  8.78 us (10%)
  Pallas kernels  2.39 us (3%)
  waiting for transfers between devices  1.37 us (1%)
  other arithmetic  1.25 us (1%)
    all_to_all x5, blocking collectives, exchange(): return lax.all_to_all(x, axis, 0, 0, tiled=True)  76.8 us
    ppermute x1, starting transfers between devices, per_device(): got = lax.ppermute(sent, 'core', [(0, 1), (1, 0)])  8.78 us
    pallas_call x5, Pallas kernels, call(): pl.pallas_call(kernel, out_shape=out_shape, compiler_params=PARAMS)(*args)  2.39 us
  transfers between devices with their start and end apart: 1, of which 1 were waited for; matrix products, arithmetic and copies ran while one was open for 0% of the time, Pallas kernels for 0%

profile of v6, /device:TPU:1, one launch (start us, length us, event | category | flops | bytes accessed | tf_op | source)
XLA Modules:
  0.0 91.8 jit_solution(15978575145326056989)
XLA Ops:
  0.6 0.0 copy-start
  0.7 1.2 %select_bitcast_fusion = bf16[32,16,512]{2,1,0:T(8,128)(2,1)S(1)} fusion(bf16[1,32,16,512]{3,2,1,0:T(8,128)(2,1)} %down_ref.1, bf16[1,32,16,512]{3,2,1,0:T(8,128)(2,1)} %up_ref.1, pred[]{:T(512)S(6)} %eq.4), kind=kLoop, calls=%fused_computation.1 | loop fusion | flops 262144 | bytes 1572865 | tf_op jit(solution)/shard_map/jit(_where)/select_n | solution.py:163
  1.9 8.8 %collective-permute-start = (bf16[32,16,512]{2,1,0:T(8,128)(2,1)S(1)}, bf16[32,16,512]{2,1,0:T(8,128)(2,1)S(1)}, u32[]{:S(2)}, u32[]{:S(2)}) collective-permute-start(bf16[32,16,512]{2,1,0:T(8,128)(2,1)S(1)} %select_bitcast_fusion), channel_id=1, source_target_pairs={{0,32},{32,0},{1,33},{33,1},{2,34},{34,2},{3,35},{35,3},{4,36},{36... | collective-permute-start | bytes 1572872 | tf_op jit(solution)/shard_map/ppermute | solution.py:164
  10.7 0.0 copy-start.3
  10.7 0.1 broadcast_select_fusion
  10.8 0.0 copy-start.2
  10.8 1.4 %collective-permute-done.got_ref = bf16[32,16,512]{2,1,0:T(8,128)(2,1)S(1)} collective-permute-done((bf16[32,16,512]{2,1,0:T(8,128)(2,1)S(1)}, bf16[32,16,512]{2,1,0:T(8,128)(2,1)S(1)}, u32[]{:S(2)}, u32[]{:S(2)}) %collective-permute-start) | collective-permute-done | bytes 524320 | tf_op jit(solution)/shard_map/ppermute | solution.py:164
  12.2 0.2 shard_map.145
  12.3 13.6 %all_to_all.25.got_ref = bf16[16,8,16,128]{3,2,1,0:T(8,128)(2,1)S(1)} all-to-all(bf16[16,8,16,128]{3,2,1,0:T(8,128)(2,1)S(1)} %shard_map.145), channel_id=1, replica_groups=mesh['x'=4,'y'=2,'core'=2,'z'=16,'h'=2] {'h','x','y'}, dimensions={0} | all-to-all | bytes 1048576 | tf_op jit(solution)/shard_map/all_to_all | solution.py:19
  26.0 0.1 shard_map.146
  26.1 0.0 copy-start.4
  26.1 24.7 %all_to_all.26 = bf16[16,16,128]{2,1,0:T(8,128)(2,1)S(1)} all-to-all(bf16[16,16,128]{2,1,0:T(8,128)(2,1)S(1)} %shard_map.146), channel_id=1, replica_groups=mesh['x'=4,'y'=2,'core'=2,'z'=16,'h'=2] {'z'}, dimensions={0} | all-to-all | bytes 131072 | tf_op jit(solution)/shard_map/all_to_all | solution.py:19
  50.7 0.3 convolution_convert_fusion
  51.0 0.0 copy-start.6
  51.0 0.0 copy-start.7
  51.0 0.0 copy-start.8
  51.0 0.0 copy-start.9
  51.0 12.0 %all_to_all.27.half_ref = bf16[16,32,128]{2,1,0:T(8,128)(2,1)S(1)} all-to-all(bf16[16,32,128]{2,1,0:T(8,128)(2,1)S(1)} %bitcast.14), channel_id=1, replica_groups=mesh['x'=4,'y'=2,'core'=2,'z'=16,'h'=2] {'x','y','core'}, dimensions={0} | all-to-all | bytes 262144 | tf_op jit(solution)/shard_map/all_to_all | solution.py:19
  63.1 0.0 copy-done.4
  63.1 0.7 shard_map.147
  63.8 8.8 %all_to_all.28.mid_ref = bf16[16,16,128]{2,1,0:T(8,128)(2,1)S(1)} all-to-all(bf16[16,16,128]{2,1,0:T(8,128)(2,1)S(1)} %get-tuple-element.15), channel_id=1, replica_groups=mesh['x'=4,'y'=2,'core'=2,'z'=16,'h'=2] {'x','y','core'}, dimensions={0} | all-to-all | bytes 131072 | tf_op jit(solution)/shard_map/all_to_all | solution.py:19
  72.6 0.6 shard_map.148
  73.1 17.7 %all_to_all.29 = bf16[32,8,128]{2,1,0:T(8,128)(2,1)S(1)} all-to-all(bf16[32,8,128]{2,1,0:T(8,128)(2,1)S(1)} %bitcast.12), channel_id=1, replica_groups=mesh['x'=4,'y'=2,'core'=2,'z'=16,'h'=2] {'z','h'}, dimensions={0} | all-to-all | bytes 131072 | tf_op jit(solution)/shard_map/all_to_all | solution.py:19
  90.9 0.9 shard_map.149
  (12 shorter events, 0.0 us)
Async XLA Ops:
  0.6 10.0 %copy-start = (bf16[1,512,512]{2,1,0:T(8,128)(2,1)S(1)}, bf16[1,512,512]{2,1,0:T(8,128)(2,1)}, u32[]{:S(2)}) copy-start(bf16[1,512,512]{2,1,0:T(8,128)(2,1)} %up_left.1) | copy-start | bytes 1572868
  0.6 10.0 %copy-start.1 = (bf16[1,512,512]{2,1,0:T(8,128)(2,1)S(1)}, bf16[1,512,512]{2,1,0:T(8,128)(2,1)}, u32[]{:S(2)}) copy-start(bf16[1,512,512]{2,1,0:T(8,128)(2,1)} %down_left.1) | copy-start | bytes 1572868
  1.9 10.3 %collective-permute-start = (bf16[32,16,512]{2,1,0:T(8,128)(2,1)S(1)}, bf16[32,16,512]{2,1,0:T(8,128)(2,1)S(1)}, u32[]{:S(2)}, u32[]{:S(2)}) collective-permute-start(bf16[32,16,512]{2,1,0:T(8,128)(2,1)S(1)} %select_bitcast_fusion), channel_id=1, source_target_pairs={{0,32},{32,0},{1,33},{33,1},{2,34},{34,2},{3,35},{35,3},{4,36},{36... | collective-permute-start | bytes 1572872 | tf_op jit(solution)/shard_map/ppermute | solution.py:164
  10.7 1.5 %copy-start.3 = (bf16[1,32,16,512]{3,2,1,0:T(8,128)(2,1)S(1)}, bf16[1,32,16,512]{3,2,1,0:T(8,128)(2,1)}, u32[]{:S(2)}) copy-start(bf16[1,32,16,512]{3,2,1,0:T(8,128)(2,1)} %down_ref.1) | copy-start | bytes 1572868
  10.8 1.4 %copy-start.2 = (bf16[1,32,16,512]{3,2,1,0:T(8,128)(2,1)S(1)}, bf16[1,32,16,512]{3,2,1,0:T(8,128)(2,1)}, u32[]{:S(2)}) copy-start(bf16[1,32,16,512]{3,2,1,0:T(8,128)(2,1)} %up_ref.1) | copy-start | bytes 1572868
  26.0 37.1 %copy-start.5 = (bf16[1,512,512]{2,1,0:T(8,128)(2,1)S(1)}, bf16[1,512,512]{2,1,0:T(8,128)(2,1)}, u32[]{:S(2)}) copy-start(bf16[1,512,512]{2,1,0:T(8,128)(2,1)} %down_right.1) | copy-start | bytes 1572868
  26.1 37.0 %copy-start.4 = (bf16[1,512,512]{2,1,0:T(8,128)(2,1)S(1)}, bf16[1,512,512]{2,1,0:T(8,128)(2,1)}, u32[]{:S(2)}) copy-start(bf16[1,512,512]{2,1,0:T(8,128)(2,1)} %up_right.1) | copy-start | bytes 1572868
  51.0 12.1 %copy-start.6 = (f32[1,32,512]{2,1,0:T(8,128)S(1)}, f32[1,32,512]{2,1,0:T(8,128)}, u32[]{:S(2)}) copy-start(f32[1,32,512]{2,1,0:T(8,128)} %up_first.1) | copy-start | bytes 196612
  51.0 12.1 %copy-start.7 = (f32[1,32,512]{2,1,0:T(8,128)S(1)}, f32[1,32,512]{2,1,0:T(8,128)}, u32[]{:S(2)}) copy-start(f32[1,32,512]{2,1,0:T(8,128)} %up_second.1) | copy-start | bytes 196612
  51.0 12.1 %copy-start.8 = (f32[1,32,512]{2,1,0:T(8,128)S(1)}, f32[1,32,512]{2,1,0:T(8,128)}, u32[]{:S(2)}) copy-start(f32[1,32,512]{2,1,0:T(8,128)} %down_first.1) | copy-start | bytes 196612
  51.0 12.1 %copy-start.9 = (f32[1,32,512]{2,1,0:T(8,128)S(1)}, f32[1,32,512]{2,1,0:T(8,128)}, u32[]{:S(2)}) copy-start(f32[1,32,512]{2,1,0:T(8,128)} %down_second.1) | copy-start | bytes 196612

commit v7 on v6

--- a/solution.py
+++ b/solution.py
@@ -11,7 +11,7 @@
 BF = jnp.bfloat16
 F32 = jnp.float32
 DP = ("x", "y", "core")
-MP = ("z", "h")
+MP = ("far", "near", "h")
 PARAMS = pltpu.CompilerParams(vmem_limit_bytes=16 * 2**20)
 
 
@@ -53,7 +53,9 @@
             for half in range(2):
                 total = total + got_ref[8 * odd + 2 * at + 1 * half].astype(F32)
         sums.append(total.reshape(16, 8, 128))
-    out_ref[...] = jnp.stack(sums, axis=1).reshape(16, 16, 128).astype(BF)
+    out = jnp.stack(sums, axis=1).reshape(2, 8, 16, 128)
+    out = jnp.stack([out[:, near] for near in range(8)])
+    out_ref[...] = out.reshape(16, 16, 128).astype(BF)
 
 
 def middle_kernel(
@@ -131,14 +133,17 @@
     top = both[:, 0].reshape(256, 128)
     low = pltpu.roll(both[:, 1].reshape(256, 128), 64, 1)
     lane = lax.broadcasted_iota(jnp.int32, (256, 128), 1)
-    out_ref[...] = jnp.where(lane < 64, top, low).reshape(16, 16, 128).astype(BF)
+    packed = jnp.where(lane < 64, top, low).reshape(2, 8, 16, 128)
+    packed = jnp.stack([packed[:, near] for near in range(8)])
+    out_ref[...] = packed.reshape(16, 16, 128).astype(BF)
 
 
 def unpack_kernel(got_ref, *refs):
     *moments, up_ref, down_ref = refs
     for own_ref, out_ref in zip(moments[:4], moments[4:]):
         out_ref[...] = own_ref[...]
-    got = got_ref[...].astype(F32).reshape(256, 128)
+    got = got_ref[...].astype(F32).reshape(8, 2, 16, 128)
+    got = jnp.stack([got[:, far] for far in range(2)]).reshape(256, 128)
     low = pltpu.roll(got, 64, 1)
     rows = jnp.stack([got.reshape(32, 8, 128), low.reshape(32, 8, 128)], axis=1)
     rows = rows.reshape(512, 128)
@@ -163,7 +168,8 @@
     sent = jnp.where(core == 0, down_partials[0], up_partials[0])
     got = lax.ppermute(sent, "core", [(0, 1), (1, 0)])
     left = jnp.where(core == 0, up_left[0], down_left[0]).reshape(32, 2, 8, 512)
-    left = lax.dynamic_index_in_dim(left, part, 1, keepdims=False).reshape(256, 512)
+    left = lax.dynamic_index_in_dim(left, part, 1, keepdims=False).reshape(2, 8, 16, 512)
+    left = left.transpose(1, 0, 2, 3).reshape(256, 512)
     got, left = lax.optimization_barrier((got, left))
     chunks = call(
         chunk_kernel,
@@ -174,7 +180,7 @@
     )
     got = exchange(chunks, ("h", "x", "y"))
     summed = call(sum_kernel, jax.ShapeDtypeStruct((16, 16, 128), BF), got)
-    grad = exchange(summed, "z").reshape(256, 128)
+    grad = exchange(summed, ("near", "far")).reshape(256, 128)
     half = jnp.einsum("pr,pq->rq", left, grad, preferred_element_type=F32)
     half = exchange(half.astype(BF).reshape(16, 32, 128), DP)
 
@@ -194,13 +200,13 @@
     packed = call(
         back_kernel, jax.ShapeDtypeStruct((16, 16, 128), BF), mid, up_left, down_left
     )
-    packed = exchange(packed.reshape(32, 8, 128), ("z", "h")).reshape(16, 16, 128)
+    packed = exchange(packed.reshape(32, 8, 128), ("near", "far", "h")).reshape(16, 16, 128)
     update = jax.ShapeDtypeStruct((32, 16, 32), BF)
     return tuple(call(unpack_kernel, [rows] * 4 + [update] * 2, packed, *moments))
 
 
 def solution(mesh):
-    mesh = Mesh(mesh.devices.reshape(4, 2, 2, 16, 2), ("x", "y", "core", "z", "h"))
+    mesh = Mesh(mesh.devices.reshape(4, 2, 2, 2, 8, 2), ("x", "y", "core", "far", "near", "h"))
     blocks, rows = P(MP, None, None), P(MP, DP, None)
     partials, update = P(DP, None, MP, None), P(None, MP, DP)
     return jax.shard_map(

time: 92.1 us -> 91.5 us (level)
  no operation moved by 1% of the time
where the time goes in v7:
time: 91.5 us; the launch traced here: 91.1 us
  blocking collectives  76.2 us (83%)
  starting transfers between devices  8.78 us (10%)
  Pallas kernels  2.39 us (3%)
  waiting for transfers between devices  1.34 us (1%)
  other arithmetic  1.25 us (1%)
    all_to_all x5, blocking collectives, exchange(): return lax.all_to_all(x, axis, 0, 0, tiled=True)  76.2 us
    ppermute x1, starting transfers between devices, per_device(): got = lax.ppermute(sent, 'core', [(0, 1), (1, 0)])  8.78 us
    pallas_call x5, Pallas kernels, call(): pl.pallas_call(kernel, out_shape=out_shape, compiler_params=PARAMS)(*args)  2.39 us
  transfers between devices with their start and end apart: 1, of which 1 were waited for; matrix products, arithmetic and copies ran while one was open for 0% of the time, Pallas kernels for 0%

profile of v7, /device:TPU:1, one launch (start us, length us, event | category | flops | bytes accessed | tf_op | source)
XLA Modules:
  0.0 91.1 jit_solution(10286560460339715949)
XLA Ops:
  0.6 0.0 copy-start
  0.7 1.2 %select_bitcast_fusion = bf16[32,16,512]{2,1,0:T(8,128)(2,1)S(1)} fusion(bf16[1,32,16,512]{3,2,1,0:T(8,128)(2,1)} %down_ref.1, bf16[1,32,16,512]{3,2,1,0:T(8,128)(2,1)} %up_ref.1, pred[]{:T(512)S(6)} %eq.4), kind=kLoop, calls=%fused_computation.1 | loop fusion | flops 262144 | bytes 1572865 | tf_op jit(solution)/shard_map/jit(_where)/select_n | solution.py:168
  1.9 8.8 %collective-permute-start = (bf16[32,16,512]{2,1,0:T(8,128)(2,1)S(1)}, bf16[32,16,512]{2,1,0:T(8,128)(2,1)S(1)}, u32[]{:S(2)}, u32[]{:S(2)}) collective-permute-start(bf16[32,16,512]{2,1,0:T(8,128)(2,1)S(1)} %select_bitcast_fusion), channel_id=1, source_target_pairs={{0,32},{32,0},{1,33},{33,1},{2,34},{34,2},{3,35},{35,3},{4,36},{36... | collective-permute-start | bytes 1572872 | tf_op jit(solution)/shard_map/ppermute | solution.py:169
  10.7 0.1 broadcast_select_fusion
  10.7 0.0 copy-start.2
  10.8 0.0 copy-start.3
  10.8 1.3 %collective-permute-done.got_ref = bf16[32,16,512]{2,1,0:T(8,128)(2,1)S(1)} collective-permute-done((bf16[32,16,512]{2,1,0:T(8,128)(2,1)S(1)}, bf16[32,16,512]{2,1,0:T(8,128)(2,1)S(1)}, u32[]{:S(2)}, u32[]{:S(2)}) %collective-permute-start) | collective-permute-done | bytes 524320 | tf_op jit(solution)/shard_map/ppermute | solution.py:169
  12.2 0.2 shard_map.145
  12.3 13.6 %all_to_all.25.got_ref = bf16[16,8,16,128]{3,2,1,0:T(8,128)(2,1)S(1)} all-to-all(bf16[16,8,16,128]{3,2,1,0:T(8,128)(2,1)S(1)} %shard_map.145), channel_id=1, replica_groups=mesh['x'=4,'y'=2,'core'=2,'far'=2,'near'=8,'h'=2] {'h','x','y'}, dimensions={0} | all-to-all | bytes 1048576 | tf_op jit(solution)/shard_map/all_to_all | solution.py:19
  26.0 0.1 shard_map.146
  26.1 0.0 copy-start.4
  26.1 25.2 %all_to_all.26 = bf16[16,16,128]{2,1,0:T(8,128)(2,1)S(1)} all-to-all(bf16[16,16,128]{2,1,0:T(8,128)(2,1)S(1)} %shard_map.146), channel_id=1, replica_groups=mesh['x'=4,'y'=2,'core'=2,'far'=2,'near'=8,'h'=2] {'near','far'}, dimensions={0} | all-to-all | bytes 131072 | tf_op jit(solution)/shard_map/all_to_all | solution.py:19
  51.3 0.3 convolution_convert_fusion
  51.5 0.0 copy-start.6
  51.6 0.0 copy-start.7
  51.6 0.0 copy-start.8
  51.6 0.0 copy-start.9
  51.6 12.1 %all_to_all.27.half_ref = bf16[16,32,128]{2,1,0:T(8,128)(2,1)S(1)} all-to-all(bf16[16,32,128]{2,1,0:T(8,128)(2,1)S(1)} %bitcast.18), channel_id=1, replica_groups=mesh['x'=4,'y'=2,'core'=2,'far'=2,'near'=8,'h'=2] {'x','y','core'}, dimensions={0} | all-to-all | bytes 262144 | tf_op jit(solution)/shard_map/all_to_all | solution.py:19
  63.7 0.0 copy-done.5
  63.7 0.7 shard_map.147
  64.4 8.8 %all_to_all.28.mid_ref = bf16[16,16,128]{2,1,0:T(8,128)(2,1)S(1)} all-to-all(bf16[16,16,128]{2,1,0:T(8,128)(2,1)S(1)} %get-tuple-element.15), channel_id=1, replica_groups=mesh['x'=4,'y'=2,'core'=2,'far'=2,'near'=8,'h'=2] {'x','y','core'}, dimensions={0} | all-to-all | bytes 131072 | tf_op jit(solution)/shard_map/all_to_all | solution.py:19
  73.2 0.6 shard_map.148
  73.7 16.5 %all_to_all.29 = bf16[32,8,128]{2,1,0:T(8,128)(2,1)S(1)} all-to-all(bf16[32,8,128]{2,1,0:T(8,128)(2,1)S(1)} %bitcast.14), channel_id=1, replica_groups=mesh['x'=4,'y'=2,'core'=2,'far'=2,'near'=8,'h'=2] {'near','far','h'}, dimensions={0} | all-to-all | bytes 131072 | tf_op jit(solution)/shard_map/all_to_all | solution.py:19
  90.2 0.9 shard_map.149
  (13 shorter events, 0.1 us)
Async XLA Ops:
  0.6 10.0 %copy-start = (bf16[1,512,512]{2,1,0:T(8,128)(2,1)S(1)}, bf16[1,512,512]{2,1,0:T(8,128)(2,1)}, u32[]{:S(2)}) copy-start(bf16[1,512,512]{2,1,0:T(8,128)(2,1)} %up_left.1) | copy-start | bytes 1572868
  0.6 10.0 %copy-start.1 = (bf16[1,512,512]{2,1,0:T(8,128)(2,1)S(1)}, bf16[1,512,512]{2,1,0:T(8,128)(2,1)}, u32[]{:S(2)}) copy-start(bf16[1,512,512]{2,1,0:T(8,128)(2,1)} %down_left.1) | copy-start | bytes 1572868
  1.9 10.3 %collective-permute-start = (bf16[32,16,512]{2,1,0:T(8,128)(2,1)S(1)}, bf16[32,16,512]{2,1,0:T(8,128)(2,1)S(1)}, u32[]{:S(2)}, u32[]{:S(2)}) collective-permute-start(bf16[32,16,512]{2,1,0:T(8,128)(2,1)S(1)} %select_bitcast_fusion), channel_id=1, source_target_pairs={{0,32},{32,0},{1,33},{33,1},{2,34},{34,2},{3,35},{35,3},{4,36},{36... | collective-permute-start | bytes 1572872 | tf_op jit(solution)/shard_map/ppermute | solution.py:169
  10.7 1.4 %copy-start.2 = (bf16[1,32,16,512]{3,2,1,0:T(8,128)(2,1)S(1)}, bf16[1,32,16,512]{3,2,1,0:T(8,128)(2,1)}, u32[]{:S(2)}) copy-start(bf16[1,32,16,512]{3,2,1,0:T(8,128)(2,1)} %up_ref.1) | copy-start | bytes 1572868
  10.8 1.4 %copy-start.3 = (bf16[1,32,16,512]{3,2,1,0:T(8,128)(2,1)S(1)}, bf16[1,32,16,512]{3,2,1,0:T(8,128)(2,1)}, u32[]{:S(2)}) copy-start(bf16[1,32,16,512]{3,2,1,0:T(8,128)(2,1)} %down_ref.1) | copy-start | bytes 1572868
  26.0 37.7 %copy-start.5 = (bf16[1,512,512]{2,1,0:T(8,128)(2,1)S(1)}, bf16[1,512,512]{2,1,0:T(8,128)(2,1)}, u32[]{:S(2)}) copy-start(bf16[1,512,512]{2,1,0:T(8,128)(2,1)} %down_right.1) | copy-start | bytes 1572868
  26.1 37.6 %copy-start.4 = (bf16[1,512,512]{2,1,0:T(8,128)(2,1)S(1)}, bf16[1,512,512]{2,1,0:T(8,128)(2,1)}, u32[]{:S(2)}) copy-start(bf16[1,512,512]{2,1,0:T(8,128)(2,1)} %up_right.1) | copy-start | bytes 1572868
  51.5 12.1 %copy-start.6 = (f32[1,32,512]{2,1,0:T(8,128)S(1)}, f32[1,32,512]{2,1,0:T(8,128)}, u32[]{:S(2)}) copy-start(f32[1,32,512]{2,1,0:T(8,128)} %up_first.1) | copy-start | bytes 196612
  51.6 12.1 %copy-start.7 = (f32[1,32,512]{2,1,0:T(8,128)S(1)}, f32[1,32,512]{2,1,0:T(8,128)}, u32[]{:S(2)}) copy-start(f32[1,32,512]{2,1,0:T(8,128)} %up_second.1) | copy-start | bytes 196612
  51.6 12.1 %copy-start.8 = (f32[1,32,512]{2,1,0:T(8,128)S(1)}, f32[1,32,512]{2,1,0:T(8,128)}, u32[]{:S(2)}) copy-start(f32[1,32,512]{2,1,0:T(8,128)} %down_first.1) | copy-start | bytes 196612
  51.6 12.1 %copy-start.9 = (f32[1,32,512]{2,1,0:T(8,128)S(1)}, f32[1,32,512]{2,1,0:T(8,128)}, u32[]{:S(2)}) copy-start(f32[1,32,512]{2,1,0:T(8,128)} %down_second.1) | copy-start | bytes 196612

commit v8 on v7

--- a/solution.py
+++ b/solution.py
@@ -119,11 +119,11 @@
                 jnp.where(lane < 32, rolled[0], rolled[1]),
                 jnp.where(lane < 96, rolled[2], rolled[3]),
             )
-            mid_ref[4 * at + w] = packed.astype(BF)
+            mid_ref[8 * (w % 2) + 2 * at + w // 2] = packed.astype(BF)
 
 
 def back_kernel(mid_ref, up_left, down_left, out_ref):
-    mid = mid_ref[...].astype(F32)
+    mid = jnp.stack([mid_ref[8 * (at % 2) + at // 2] for at in range(16)]).astype(F32)
     other = pltpu.roll(mid.reshape(256, 128), 64, 1).reshape(16, 16, 128)
     mid = jnp.stack([mid, other], axis=1).reshape(512, 128).astype(BF)
     up = jnp.dot(up_left[0], mid, preferred_element_type=F32)
@@ -196,7 +196,7 @@
         down_first,
         down_second,
     )
-    mid = exchange(mid, DP)
+    mid = exchange(mid, ("core", "x", "y"))
     packed = call(
         back_kernel, jax.ShapeDtypeStruct((16, 16, 128), BF), mid, up_left, down_left
     )

time: 91.5 us -> 91.4 us (level)
  no operation moved by 1% of the time
where the time goes in v8:
time: 91.4 us; the launch traced here: 91 us
  blocking collectives  76 us (83%)
  starting transfers between devices  8.78 us (10%)
  Pallas kernels  2.39 us (3%)
  waiting for transfers between devices  1.34 us (1%)
  other arithmetic  1.25 us (1%)
    all_to_all x5, blocking collectives, exchange(): return lax.all_to_all(x, axis, 0, 0, tiled=True)  76 us
    ppermute x1, starting transfers between devices, per_device(): got = lax.ppermute(sent, 'core', [(0, 1), (1, 0)])  8.78 us
    pallas_call x5, Pallas kernels, call(): pl.pallas_call(kernel, out_shape=out_shape, compiler_params=PARAMS)(*args)  2.39 us
  transfers between devices with their start and end apart: 1, of which 1 were waited for; matrix products, arithmetic and copies ran while one was open for 0% of the time, Pallas kernels for 0%

profile of v8, /device:TPU:1, one launch (start us, length us, event | category | flops | bytes accessed | tf_op | source)
XLA Modules:
  0.0 91.0 jit_solution(17941821729850816827)
XLA Ops:
  0.6 0.0 copy-start
  0.6 0.0 copy-start.1
  0.7 1.2 %select_bitcast_fusion = bf16[32,16,512]{2,1,0:T(8,128)(2,1)S(1)} fusion(bf16[1,32,16,512]{3,2,1,0:T(8,128)(2,1)} %down_ref.1, bf16[1,32,16,512]{3,2,1,0:T(8,128)(2,1)} %up_ref.1, pred[]{:T(512)S(6)} %eq.4), kind=kLoop, calls=%fused_computation.1 | loop fusion | flops 262144 | bytes 1572865 | tf_op jit(solution)/shard_map/jit(_where)/select_n | solution.py:168
  1.9 8.8 %collective-permute-start = (bf16[32,16,512]{2,1,0:T(8,128)(2,1)S(1)}, bf16[32,16,512]{2,1,0:T(8,128)(2,1)S(1)}, u32[]{:S(2)}, u32[]{:S(2)}) collective-permute-start(bf16[32,16,512]{2,1,0:T(8,128)(2,1)S(1)} %select_bitcast_fusion), channel_id=1, source_target_pairs={{0,32},{32,0},{1,33},{33,1},{2,34},{34,2},{3,35},{35,3},{4,36},{36... | collective-permute-start | bytes 1572872 | tf_op jit(solution)/shard_map/ppermute | solution.py:169
  10.7 0.1 broadcast_select_fusion
  10.7 0.0 copy-start.2
  10.8 0.0 copy-start.3
  10.8 1.3 %collective-permute-done.got_ref = bf16[32,16,512]{2,1,0:T(8,128)(2,1)S(1)} collective-permute-done((bf16[32,16,512]{2,1,0:T(8,128)(2,1)S(1)}, bf16[32,16,512]{2,1,0:T(8,128)(2,1)S(1)}, u32[]{:S(2)}, u32[]{:S(2)}) %collective-permute-start) | collective-permute-done | bytes 524320 | tf_op jit(solution)/shard_map/ppermute | solution.py:169
  12.2 0.2 shard_map.145
  12.3 13.6 %all_to_all.25.got_ref = bf16[16,8,16,128]{3,2,1,0:T(8,128)(2,1)S(1)} all-to-all(bf16[16,8,16,128]{3,2,1,0:T(8,128)(2,1)S(1)} %shard_map.145), channel_id=1, replica_groups=mesh['x'=4,'y'=2,'core'=2,'far'=2,'near'=8,'h'=2] {'h','x','y'}, dimensions={0} | all-to-all | bytes 1048576 | tf_op jit(solution)/shard_map/all_to_all | solution.py:19
  26.0 0.1 shard_map.146
  26.1 0.0 copy-start.4
  26.1 25.2 %all_to_all.26 = bf16[16,16,128]{2,1,0:T(8,128)(2,1)S(1)} all-to-all(bf16[16,16,128]{2,1,0:T(8,128)(2,1)S(1)} %shard_map.146), channel_id=1, replica_groups=mesh['x'=4,'y'=2,'core'=2,'far'=2,'near'=8,'h'=2] {'near','far'}, dimensions={0} | all-to-all | bytes 131072 | tf_op jit(solution)/shard_map/all_to_all | solution.py:19
  51.3 0.3 convolution_convert_fusion
  51.5 0.0 copy-start.6
  51.6 0.0 copy-start.7
  51.6 0.0 copy-start.8
  51.6 0.0 copy-start.9
  51.6 12.1 %all_to_all.27.half_ref = bf16[16,32,128]{2,1,0:T(8,128)(2,1)S(1)} all-to-all(bf16[16,32,128]{2,1,0:T(8,128)(2,1)S(1)} %bitcast.18), channel_id=1, replica_groups=mesh['x'=4,'y'=2,'core'=2,'far'=2,'near'=8,'h'=2] {'x','y','core'}, dimensions={0} | all-to-all | bytes 262144 | tf_op jit(solution)/shard_map/all_to_all | solution.py:19
  63.7 0.7 shard_map.147
  64.4 8.6 %all_to_all.28.mid_ref = bf16[16,16,128]{2,1,0:T(8,128)(2,1)S(1)} all-to-all(bf16[16,16,128]{2,1,0:T(8,128)(2,1)S(1)} %get-tuple-element.15), channel_id=1, replica_groups=mesh['x'=4,'y'=2,'core'=2,'far'=2,'near'=8,'h'=2] {'core','x','y'}, dimensions={0} | all-to-all | bytes 131072 | tf_op jit(solution)/shard_map/all_to_all | solution.py:19
  73.0 0.6 shard_map.148
  73.5 16.6 %all_to_all.29 = bf16[32,8,128]{2,1,0:T(8,128)(2,1)S(1)} all-to-all(bf16[32,8,128]{2,1,0:T(8,128)(2,1)S(1)} %bitcast.14), channel_id=1, replica_groups=mesh['x'=4,'y'=2,'core'=2,'far'=2,'near'=8,'h'=2] {'near','far','h'}, dimensions={0} | all-to-all | bytes 131072 | tf_op jit(solution)/shard_map/all_to_all | solution.py:19
  90.1 0.9 shard_map.149
  (13 shorter events, 0.1 us)
Async XLA Ops:
  0.6 10.0 %copy-start = (bf16[1,512,512]{2,1,0:T(8,128)(2,1)S(1)}, bf16[1,512,512]{2,1,0:T(8,128)(2,1)}, u32[]{:S(2)}) copy-start(bf16[1,512,512]{2,1,0:T(8,128)(2,1)} %up_left.1) | copy-start | bytes 1572868
  0.6 10.0 %copy-start.1 = (bf16[1,512,512]{2,1,0:T(8,128)(2,1)S(1)}, bf16[1,512,512]{2,1,0:T(8,128)(2,1)}, u32[]{:S(2)}) copy-start(bf16[1,512,512]{2,1,0:T(8,128)(2,1)} %down_left.1) | copy-start | bytes 1572868
  1.9 10.3 %collective-permute-start = (bf16[32,16,512]{2,1,0:T(8,128)(2,1)S(1)}, bf16[32,16,512]{2,1,0:T(8,128)(2,1)S(1)}, u32[]{:S(2)}, u32[]{:S(2)}) collective-permute-start(bf16[32,16,512]{2,1,0:T(8,128)(2,1)S(1)} %select_bitcast_fusion), channel_id=1, source_target_pairs={{0,32},{32,0},{1,33},{33,1},{2,34},{34,2},{3,35},{35,3},{4,36},{36... | collective-permute-start | bytes 1572872 | tf_op jit(solution)/shard_map/ppermute | solution.py:169
  10.7 1.4 %copy-start.2 = (bf16[1,32,16,512]{3,2,1,0:T(8,128)(2,1)S(1)}, bf16[1,32,16,512]{3,2,1,0:T(8,128)(2,1)}, u32[]{:S(2)}) copy-start(bf16[1,32,16,512]{3,2,1,0:T(8,128)(2,1)} %up_ref.1) | copy-start | bytes 1572868
  10.8 1.4 %copy-start.3 = (bf16[1,32,16,512]{3,2,1,0:T(8,128)(2,1)S(1)}, bf16[1,32,16,512]{3,2,1,0:T(8,128)(2,1)}, u32[]{:S(2)}) copy-start(bf16[1,32,16,512]{3,2,1,0:T(8,128)(2,1)} %down_ref.1) | copy-start | bytes 1572868
  26.0 37.7 %copy-start.5 = (bf16[1,512,512]{2,1,0:T(8,128)(2,1)S(1)}, bf16[1,512,512]{2,1,0:T(8,128)(2,1)}, u32[]{:S(2)}) copy-start(bf16[1,512,512]{2,1,0:T(8,128)(2,1)} %down_right.1) | copy-start | bytes 1572868
  26.1 37.6 %copy-start.4 = (bf16[1,512,512]{2,1,0:T(8,128)(2,1)S(1)}, bf16[1,512,512]{2,1,0:T(8,128)(2,1)}, u32[]{:S(2)}) copy-start(bf16[1,512,512]{2,1,0:T(8,128)(2,1)} %up_right.1) | copy-start | bytes 1572868
  51.5 12.1 %copy-start.6 = (f32[1,32,512]{2,1,0:T(8,128)S(1)}, f32[1,32,512]{2,1,0:T(8,128)}, u32[]{:S(2)}) copy-start(f32[1,32,512]{2,1,0:T(8,128)} %up_first.1) | copy-start | bytes 196612
  51.6 12.1 %copy-start.7 = (f32[1,32,512]{2,1,0:T(8,128)S(1)}, f32[1,32,512]{2,1,0:T(8,128)}, u32[]{:S(2)}) copy-start(f32[1,32,512]{2,1,0:T(8,128)} %up_second.1) | copy-start | bytes 196612
  51.6 12.1 %copy-start.8 = (f32[1,32,512]{2,1,0:T(8,128)S(1)}, f32[1,32,512]{2,1,0:T(8,128)}, u32[]{:S(2)}) copy-start(f32[1,32,512]{2,1,0:T(8,128)} %down_first.1) | copy-start | bytes 196612
  51.6 12.1 %copy-start.9 = (f32[1,32,512]{2,1,0:T(8,128)S(1)}, f32[1,32,512]{2,1,0:T(8,128)}, u32[]{:S(2)}) copy-start(f32[1,32,512]{2,1,0:T(8,128)} %down_second.1) | copy-start | bytes 196612
